TPU v7x, 32 devices: a whole 2x2x4 slice. The times are simulated.
32 devices in a mesh: groups: 2 (over y), seq: 4 (over z), dp: 4 (over x, core).
Axes of the slice: x: 2, y: 2, z: 4, core: 2. Of those that a mesh axis runs over, the one named last changes fastest.
Arguments:
- acceptance_gate: bfloat16 [8, 512, 1280], P(('groups', 'dp'), 'seq'), parts along dimension 0, may hold values from -6 to 6
- logarithmic_fade_factor: bfloat16 [8, 512, 1280], P(('groups', 'dp'), 'seq'), parts along dimension 0, may hold values from -12 to 0
- probe_matrix: bfloat16 [8, 512, 1280], P(('groups', 'dp'), 'seq'), parts along dimension 0, may hold values from -0.75 to 0.75
- payload_matrix: bfloat16 [8, 512, 1280], P(('groups', 'dp'), 'seq'), parts along dimension 0, may hold values from -6 to 6
- erasure_vector: bfloat16 [8, 512, 1280], P(('groups', 'dp'), 'seq'), parts along dimension 0, may hold values from -6 to 6
- inplace_update_step: bfloat16 [8, 512, 1280], P(('groups', 'dp'), 'seq'), parts along dimension 0, may hold values from 0.0079956055 to 0.019897461
- extra_probe_factor: float32 [1280], replicated, may hold values from -3 to 3
- group_scaling_factor: float32 [1280], replicated, may hold values from 0.5 to 1.5
Outputs:
- blended_signal: bfloat16 [8, 512, 1280], P(('groups', 'dp'), 'seq'), parts along dimension 0
- final_state: float32 [8, 1280, 64], P(('groups', 'dp'), 'seq'), parts along dimension 0
There are 2 independent parts, one for each index of `groups`. A program takes and returns all parts, laid end to end along the dimension named above; an argument that names none is the same for every part. Nothing has to cross between parts.
All inputs are finite; a program needn't handle non-finite values.
Results may differ from a plain program's by a relative error of at most 0.001.
Values sent between devices are 32-bit elements; how exact they have to be, the bound alone decides.
A program may use at most 64 MiB of HBM per device.

v0:
```python
import jax
import jax.numpy as jnp
from jax import lax
from jax.sharding import PartitionSpec as P

GROUP_DIMENSION = 64
BLOCK = 64


HIGHEST_PRECISION = lax.Precision.HIGHEST
SCORE_PRECISION = lax.Precision.HIGH
KEY_EPS = 1e-05
NORM_EPS = 0.00064


def passed_along(shard, axis, by):
    devices = lax.axis_size(axis)
    pairs = [(i, i + by) for i in range(devices) if 0 <= i + by < devices]
    return lax.ppermute(shard, axis, pairs)


def broadcast(value, axis, source):
    kept = jnp.where(lax.axis_index(axis) == source, value, 0).astype(value.dtype)
    return lax.psum(kept, axis)


def contract(form, left_side, right_side):
    return jnp.einsum(form, left_side, right_side, precision=HIGHEST_PRECISION)


def contract_score(form, left_side, right_side):
    return jnp.einsum(form, left_side, right_side, precision=SCORE_PRECISION)


def apply_map(state_now, state_map):
    return contract("bhvk,bhkj->bhvj", state_now, state_map)


def local_pass(
    acceptance_gate,
    logarithmic_fade_factor,
    probe_matrix,
    payload_matrix,
    erasure_vector,
    inplace_update_step,
):
    symbol_entries, feature_total = acceptance_gate.shape
    blocks = symbol_entries // BLOCK
    group_total = feature_total // GROUP_DIMENSION

    def heads_first(array):
        return jnp.transpose(
            array.reshape(blocks, BLOCK, group_total, GROUP_DIMENSION), (0, 2, 1, 3)
        ).astype(jnp.float32)

    reader_in = heads_first(acceptance_gate)
    key_vals = heads_first(probe_matrix)
    values_h = heads_first(payload_matrix)
    log_step = -jnp.exp(heads_first(logarithmic_fade_factor))
    removal = heads_first(erasure_vector)
    kappa = (
        removal
        * lax.rsqrt(jnp.mean(removal * removal, -1, keepdims=True) + KEY_EPS)
        * GROUP_DIMENSION ** (-0.5)
    )
    away_dir = kappa * heads_first(inplace_update_step)
    row_ids = lax.broadcasted_iota(jnp.int32, (BLOCK, BLOCK), 0)
    col_ids = lax.broadcasted_iota(jnp.int32, (BLOCK, BLOCK), 1)
    inclusive = (row_ids >= col_ids).astype(jnp.float32)
    strict = (row_ids > col_ids).astype(jnp.float32)
    cumulative = jnp.cumsum(log_step, axis=2)
    before = cumulative - log_step
    toward_dec = -kappa * jnp.exp(before)
    reader_dec = reader_in * jnp.exp(cumulative)
    away_inv = away_dir * jnp.exp(-cumulative)
    keys_inv = key_vals * jnp.exp(-cumulative)
    gamma_end = jnp.exp(cumulative[:, :, -1])
    query_sides = jnp.concatenate([toward_dec, reader_dec], 2)
    key_sides = jnp.concatenate([away_inv, keys_inv], 2)
    scores = contract_score("nhtc,nhsc->nhts", query_sides, key_sides)
    mix_away = scores[:, :, :BLOCK, :BLOCK] * strict
    mix_keys = scores[:, :, :BLOCK, BLOCK:] * strict
    read_away = scores[:, :, BLOCK:, :BLOCK] * inclusive
    read_keys = scores[:, :, BLOCK:, BLOCK:] * inclusive
    known_side = jnp.concatenate(
        [toward_dec, contract_score("nhts,nhsc->nhtc", mix_keys, values_h)], -1
    )
    system = jnp.eye(BLOCK, dtype=jnp.float32) - mix_away
    solved = lax.linalg.triangular_solve(
        system, known_side, left_side=True, lower=True, unit_diagonal=True
    )
    from_state = solved[..., :GROUP_DIMENSION]
    from_values = solved[..., GROUP_DIMENSION:]
    unit_map = jnp.eye(GROUP_DIMENSION, dtype=jnp.float32)
    transition = (unit_map + contract("nhsk,nhsj->nhkj", from_state, away_inv)) * gamma_end[
        :, :, None, :
    ]
    contribution = (
        contract("nhsv,nhsj->nhvj", from_values, away_inv)
        + contract("nhsv,nhsj->nhvj", values_h, keys_inv)
    ) * gamma_end[:, :, None, :]
    reader = reader_dec + contract_score("nhts,nhsk->nhtk", read_away, from_state)
    within_split = contract_score("nhts,nhsv->nhtv", read_away, from_values) + contract_score(
        "nhts,nhsv->nhtv", read_keys, values_h
    )

    def advance_block(carried, pieces):
        map_so_far, add_so_far = carried
        step_map, step_add = pieces
        updated = (
            contract("hmk,hkj->hmj", map_so_far, step_map),
            contract("hvk,hkj->hvj", add_so_far, step_map) + step_add,
        )
        return (updated, (map_so_far, add_so_far))

    initial = (
        jnp.broadcast_to(unit_map, (group_total, GROUP_DIMENSION, GROUP_DIMENSION)),
        jnp.zeros((group_total, GROUP_DIMENSION, GROUP_DIMENSION), jnp.float32),
    )
    totals, priors = lax.scan(advance_block, initial, (transition, contribution))
    lifted_state = contract("nhtk,nhmk->nhtm", reader, priors[0])
    within_split = within_split + contract("nhtk,nhvk->nhtv", reader, priors[1])
    return (lifted_state, within_split, totals[1], totals[0])


def finish_output(
    lifted_state,
    within_split,
    incoming_state,
    acceptance_gate,
    probe_matrix,
    payload_matrix,
    extra_probe_factor,
    group_scaling_factor,
):
    symbol_entries, feature_total = acceptance_gate.shape
    group_total = feature_total // GROUP_DIMENSION
    result = within_split + contract("nhtm,hvm->nhtv", lifted_state, incoming_state)
    result = jnp.transpose(result, (0, 2, 1, 3)).reshape(
        symbol_entries, group_total, GROUP_DIMENSION
    )
    average = jnp.mean(result, -1, keepdims=True)
    centered = result - average
    spread = jnp.mean(centered * centered, -1, keepdims=True)
    standardized_result = (
        centered
        * lax.rsqrt(spread + NORM_EPS)
        * group_scaling_factor.reshape(group_total, GROUP_DIMENSION)
    )
    receptance_per_head = acceptance_gate.astype(jnp.float32).reshape(
        symbol_entries, group_total, GROUP_DIMENSION
    )
    key_per_head = probe_matrix.astype(jnp.float32).reshape(
        symbol_entries, group_total, GROUP_DIMENSION
    )
    value_per_head = payload_matrix.astype(jnp.float32).reshape(
        symbol_entries, group_total, GROUP_DIMENSION
    )
    extra_result = (
        jnp.sum(
            receptance_per_head
            * key_per_head
            * extra_probe_factor.reshape(group_total, GROUP_DIMENSION),
            -1,
            keepdims=True,
        )
        * value_per_head
    )
    return (
        (standardized_result + extra_result)
        .reshape(symbol_entries, feature_total)
        .astype(jnp.bfloat16)
    )


def on_device(
    acceptance_gate,
    logarithmic_fade_factor,
    probe_matrix,
    payload_matrix,
    erasure_vector,
    inplace_update_step,
    extra_probe_factor,
    group_scaling_factor,
):
    lifted_state, within_split, local_add, local_map = jax.vmap(local_pass)(
        acceptance_gate,
        logarithmic_fade_factor,
        probe_matrix,
        payload_matrix,
        erasure_vector,
        inplace_update_step,
    )
    members = lax.axis_size("seq")
    nothing = jnp.zeros_like(local_add)

    def relay(turn_index, carried):
        incoming = passed_along(carried[1], "seq", 1)
        return (incoming, apply_map(incoming, local_map) + local_add)

    incoming_state, leaving = lax.fori_loop(0, members - 1, relay, (nothing, local_add))
    closing = broadcast(leaving, "seq", members - 1)
    series_entries = closing.shape[0]
    flat_state = closing.reshape(series_entries, -1, GROUP_DIMENSION)
    slice_rows = flat_state.shape[1] // members
    final_state = lax.dynamic_slice_in_dim(
        flat_state, lax.axis_index("seq") * slice_rows, slice_rows, 1
    )
    blended_signal = jax.vmap(finish_output, in_axes=(0, 0, 0, 0, 0, 0, None, None))(
        lifted_state,
        within_split,
        incoming_state,
        acceptance_gate,
        probe_matrix,
        payload_matrix,
        extra_probe_factor,
        group_scaling_factor,
    )
    return (blended_signal, final_state)


def solution(mesh):
    in_specs = (
        P(("groups", "dp"), "seq", None),
        P(("groups", "dp"), "seq", None),
        P(("groups", "dp"), "seq", None),
        P(("groups", "dp"), "seq", None),
        P(("groups", "dp"), "seq", None),
        P(("groups", "dp"), "seq", None),
        P(),
        P(),
    )
    out_specs = (P(("groups", "dp"), "seq", None), P(("groups", "dp"), "seq", None))
    return jax.shard_map(
        on_device, mesh=mesh, in_specs=in_specs, out_specs=out_specs, check_vma=False
    )
```

profile of v0, /device:TPU:18, one launch (start us, length us, event | category | flops | bytes accessed | tf_op | source)
XLA Modules:
  0.0 382.7 jit_solution(7529248392724634668)
XLA Ops:
  7.3 1.1 exponential_negate_fusion
  9.2 1.7 copy.90
  10.9 1.5 fusion.73
  12.4 1.5 copy.91
  14.4 1.5 copy.96
  15.9 1.6 reshape.387
  17.5 1.8 copy.87
  19.6 1.0 copy-done.30
  20.8 1.9 reshape.385
  22.7 1.2 copy.92
  23.9 1.8 reshape.383
  26.8 3.7 fusion.48
  30.6 2.4 convolution_bitcast_fusion.4
  32.9 3.0 convolution_bitcast_fusion.2
  35.9 2.0 convolution_bitcast_fusion.5
  37.9 1.6 fusion.34
  39.5 198.0 %custom-call.3 = f32[1,2,20,1,64,64]{4,5,3,2,1,0:T(8,128)} custom-call(f32[1,2,20,1,64,64]{5,4,3,2,1,0:T(8,128)} %fusion.34), custom_call_target="InvertDiagBlocksLowerTriangular" | custom-call | tf_op jit(solution)/shard_map/vmap()/triangular_solve | solution.py:89
  237.5 7.0 %fusion.19 = f32[1,2,20,64,128]{4,3,2,1,0:T(8,128)S(1)} fusion(f32[1,2,20,64,64]{3,4,2,1,0:T(8,128)} %convolution_bitcast_fusion.5, f32[1,2,20,64,64]{3,4,2,1,0:T(8,128)S(1)} %copy-done.12, f32[1,2,20,1,64,64]{4,5,3,2,1,0:T(8,128)} %custom-call.3), kind=kOutput, calls=%fused_computation.34 | convolution fusion | flops 251985920 | bytes 3276800 | tf_op jit(solution)/shard_map/vmap()/triangular_solve | solution.py:89
  244.5 2.4 fusion.20
  246.9 3.9 %fusion.21 = f32[2,1,20,64,64]{4,3,2,0,1:T(8,128)} fusion(f32[2,20,64,64]{3,2,1,0:T(8,128)S(1)} %copy-done.15, f32[1,2,20,64,64]{3,4,2,1,0:T(8,128)S(1)} %get-tuple-element.141, f32[1,2,20,64,128]{4,3,2,1,0:T(8,128)S(1)} %fusion.19, f32[2,20,64]{2,1,0:T(8,128)S(1)} %fusion.69), kind=kOutput, calls=%fused_computation.36 | convolution fusion | flops 126156800 | bytes 3287040 | tf_op jit(solution)/shard_map/vmap(nhsv,nhsj->nhvj)/dot_general | solution.py:28
  250.9 0.9 broadcast.123.clone
  251.8 13.4 %while.30 = (s32[]{:T(128)}, f32[1,20,64,64]{2,3,1,0:T(8,128)S(1)}, f32[1,20,64,64]{2,3,1,0:T(8,128)}, f32[2,1,20,64,64]{3,4,2,1,0:T(8,128)}, f32[2,1,20,64,64]{...) while((s32[]{:T(128)}, f32[1,20,64,64]{2,3,1,0:T(8,128)S(1)}, ...), condition=%wide.region_3.4_spmd.clone, body=%wide.region_2.3_spmd.sunk.clone | while | flops 125911040 | bytes 23593228 | solution.py:120
  251.8 1.2 copy.215
  253.9 2.1 convolution_bitcast_fusion.9
  256.4 2.0 fusion.97
  258.5 1.2 copy.215
  260.6 2.1 convolution_bitcast_fusion.9
  263.2 2.0 fusion.97
  265.2 1.3 copy.120
  266.9 64.8 %while.31 = (s32[]{:T(128)}, f32[1,20,64,64]{3,2,1,0:T(8,128)}, f32[1,20,64,64]{3,2,1,0:T(8,128)S(1)}, f32[1,20,64,64]{3,2,1,0:T(8,128)S(1)}, f32[1,20,64,64]{3,2,1,0:T(8,128)S(1)}) while((s32[]{:T(128)}, f32[1,20,64,64]{3,2,1,0:T(8,128)}, f32[1,20,64,64]{3,2,1,0:T(8,128)S(1)}, f32[1,20,64,64]{3,2,1,0:T(8,128)S(1)}, ...), condition=%wide.region_5.6_spmd.clone, body=%wide.region_4.5_spmd.sunk.clone | while | flops 62996480 | bytes 3932289 | solution.py:201
  266.9 3.6 collective-permute-start
  270.5 14.9 %collective-permute-done = f32[1,20,64,64]{3,2,1,0:T(8,128)S(1)} collective-permute-done((f32[1,20,64,64]{3,2,1,0:T(8,128)S(1)}, f32[1,20,64,64]{3,2,1,0:T(8,128)S(1)}, u32[]{:S(2)}, u32[]{:S(2)}) %collective-permute-start) | collective-permute-done | bytes 327712 | tf_op jit(solution)/shard_map/while/body/eval_jaxpr/ppermute | solution.py:19
  286.2 3.5 collective-permute-start
  289.7 14.0 %collective-permute-done = f32[1,20,64,64]{3,2,1,0:T(8,128)S(1)} collective-permute-done((f32[1,20,64,64]{3,2,1,0:T(8,128)S(1)}, f32[1,20,64,64]{3,2,1,0:T(8,128)S(1)}, u32[]{:S(2)}, u32[]{:S(2)}) %collective-permute-start) | collective-permute-done | bytes 327712 | tf_op jit(solution)/shard_map/while/body/eval_jaxpr/ppermute | solution.py:19
  304.5 3.5 collective-permute-start
  308.0 13.1 %collective-permute-done = f32[1,20,64,64]{3,2,1,0:T(8,128)S(1)} collective-permute-done((f32[1,20,64,64]{3,2,1,0:T(8,128)S(1)}, f32[1,20,64,64]{3,2,1,0:T(8,128)S(1)}, u32[]{:S(2)}, u32[]{:S(2)}) %collective-permute-start) | collective-permute-done | bytes 327712 | tf_op jit(solution)/shard_map/while/body/eval_jaxpr/ppermute | solution.py:19
  332.6 1.0 broadcast_select_fusion
  333.5 2.1 copy.158
  335.7 0.9 fusion.27
  337.4 1.2 fusion.25
  339.6 1.6 convolution_add_fusion.4
  341.3 2.3 fusion.40
  343.6 2.3 fusion.16
  346.0 3.9 %fusion.72 = (f32[2,64,20]{1,2,0:T(8,128)S(1)}, f32[1,2,64,20,64]{2,4,3,1,0:T(8,128)S(1)}) fusion(f32[1,2,20,64,64]{3,4,2,1,0:T(8,128)S(1)} %fusion.16, f32[2,20,64,64]{3,2,0,1:T(8,128)S(1)} %fusion.40, f32[1,20,64,64]{3,2,1,0:T(8,128)S(1)} %copy-done.6), kind=kOutput, calls=%fused_computation.118 | convolution fusion | flops 126154240 | bytes 2304000 | tf_op jit(solution)/shard_map/vmap(nhtm,hvm->nhtv)/dot_general | solution.py:28
  349.8 1.0 copy.126
  352.8 0.9 copy.131
  353.7 20.3 %all-reduce.2.cloned.1.call-done = f32[1,1280,64]{1,2,0:T(8,128)} async-done(((f32[1,1280,64]{1,2,0:T(8,128)}), f32[1,1280,64]{1,2,0:T(8,128)}) %all-reduce.2.cloned.1.call-update) | async-done | bytes 327696 | tf_op jit(solution)/shard_map/psum | solution.py:24
  374.0 1.6 constant_dynamic-slice_fusion.1
  (132 shorter events, 12.7 us)
Async XLA Ops:
  7.2 366.8 %all-reduce.2.cloned.1.call-start = ((), (), s32[]{:S(2)}) async-start(), calls=%async_computation | async-start | bytes 655360 | tf_op jit(solution)/shard_map/psum | solution.py:24
  12.4 1.5 copy-start.32
  14.4 1.5 copy-start.33
  19.4 3.4 copy-start.8
  19.4 1.2 copy-start.30
  20.8 5.0 %copy-start.16 = (bf16[1,128,1280]{1,2,0:T(8,128)(2,1)}, bf16[1,128,1280]{1,2,0:T(8,128)(2,1)S(1)}, u32[]{:S(2)}) copy-start(bf16[1,128,1280]{1,2,0:T(8,128)(2,1)S(1)} %copy.98) | copy-start | bytes 983044
  23.9 2.4 copy-start.18
  23.9 1.9 copy-start.31
  26.0 0.7 copy-start.20
  26.3 9.6 %copy-start.13 = (bf16[1,2,64,20,64]{2,1,4,3,0:T(2,128)(2,1)}, bf16[1,2,64,20,64]{2,1,4,3,0:T(2,128)(2,1)S(1)}, u32[]{:S(2)}) copy-start(bf16[1,2,64,20,64]{2,1,4,3,0:T(2,128)(2,1)S(1)} %reshape.368) | copy-start | bytes 983044
  30.5 2.4 copy-start.9
  30.5 2.4 copy-start.11
  35.9 2.0 copy-start.2
  37.9 199.6 %copy-start.12 = (f32[1,2,20,64,64]{3,4,2,1,0:T(8,128)S(1)}, f32[1,2,20,64,64]{3,4,2,1,0:T(8,128)}, u32[]{:S(2)}) copy-start(f32[1,2,20,64,64]{3,4,2,1,0:T(8,128)} %copy-done.11) | copy-start | bytes 1966084
  244.5 2.4 copy-start
  244.5 2.4 copy-start.15
  251.8 1.5 copy-start.24
  251.8 1.9 copy-start.27
  253.8 2.1 copy-start.25
  253.9 2.1 copy-start.28
  253.9 2.3 copy-start.7
  256.4 2.1 copy-start.4
  258.5 1.5 copy-start.24
  258.5 1.9 copy-start.27
  260.6 2.1 copy-start.25
  260.6 2.1 copy-start.28
  260.6 2.3 copy-start.7
  263.2 2.1 copy-start.4
  266.8 68.9 %copy-start.14 = (bf16[1,2,64,20,64]{2,1,4,3,0:T(2,128)(2,1)S(1)}, bf16[1,2,64,20,64]{2,1,4,3,0:T(2,128)(2,1)}, u32[]{:S(2)}) copy-start(bf16[1,2,64,20,64]{2,1,4,3,0:T(2,128)(2,1)} %copy-done.13) | copy-start | bytes 983044
  266.9 18.5 %collective-permute-start = (f32[1,20,64,64]{3,2,1,0:T(8,128)S(1)}, f32[1,20,64,64]{3,2,1,0:T(8,128)S(1)}, u32[]{:S(2)}, u32[]{:S(2)}) collective-permute-start(f32[1,20,64,64]{3,2,1,0:T(8,128)S(1)} %get-tuple-element.284), channel_id=1, source_target_pairs={{0,4},{4,8},{8,12},{1,5},{5,9},{9,13},{2,6},{6,10},{10,14},{3,7},{... | collective-permute-start | bytes 983048 | tf_op jit(solution)/shard_map/while/body/eval_jaxpr/ppermute | solution.py:19
  285.4 0.8 copy-start.5
  286.2 17.5 %collective-permute-start = (f32[1,20,64,64]{3,2,1,0:T(8,128)S(1)}, f32[1,20,64,64]{3,2,1,0:T(8,128)S(1)}, u32[]{:S(2)}, u32[]{:S(2)}) collective-permute-start(f32[1,20,64,64]{3,2,1,0:T(8,128)S(1)} %get-tuple-element.284), channel_id=1, source_target_pairs={{0,4},{4,8},{8,12},{1,5},{5,9},{9,13},{2,6},{6,10},{10,14},{3,7},{... | collective-permute-start | bytes 983048 | tf_op jit(solution)/shard_map/while/body/eval_jaxpr/ppermute | solution.py:19
  303.7 0.8 copy-start.5
  304.5 16.6 %collective-permute-start = (f32[1,20,64,64]{3,2,1,0:T(8,128)S(1)}, f32[1,20,64,64]{3,2,1,0:T(8,128)S(1)}, u32[]{:S(2)}, u32[]{:S(2)}) collective-permute-start(f32[1,20,64,64]{3,2,1,0:T(8,128)S(1)} %get-tuple-element.284), channel_id=1, source_target_pairs={{0,4},{4,8},{8,12},{1,5},{5,9},{9,13},{2,6},{6,10},{10,14},{3,7},{... | collective-permute-start | bytes 983048 | tf_op jit(solution)/shard_map/while/body/eval_jaxpr/ppermute | solution.py:19
  321.1 0.8 copy-start.5
  331.7 0.9 copy-start.23
  332.6 3.1 copy-start.3
  335.7 1.3 copy-start.1
  335.7 1.7 copy-start.10
  337.4 1.2 copy-start.17
  337.4 1.3 copy-start.19
  339.6 1.6 copy-start.29
  341.2 2.3 copy-start.26
  343.6 2.3 copy-start.6
  351.2 0.8 copy-start.35
  351.2 1.1 copy-start.22
  351.2 1.3 copy-start.21
  351.2 1.3 copy-start.34
Sparse Core Ops, SparseCore 0:
  335.8 38.1 all-reduce.1
where the time goes:
time: 389 us; the launch traced here: 383 us
  other arithmetic  209 us (54%)
  waiting for transfers between devices  62.2 us (16%)
  matrix products  43.5 us (11%)
  local copies, waits for them, and re-layouts  32.7 us (8%)
  between operations  14.8 us (4%)
  starting transfers between devices  10.6 us (3%)
  loops' own time  9.93 us (3%)
    another operation x4, other arithmetic, local_pass(): lax.linalg.triangular_solve(system, known_side, left_side=True, lower=Tru...  200 us
    ppermute x3, waiting for transfers between devices, passed_along(): return lax.ppermute(shard, axis, pairs)  42 us
    dot_general x13, matrix products, contract(): return jnp.einsum(form, left_side, right_side, precision=HIGHEST_PRECISION)  27.7 us
    psum x1, waiting for transfers between devices, broadcast(): return lax.psum(kept, axis)  20.3 us
    ppermute x3, starting transfers between devices, passed_along(): return lax.ppermute(shard, axis, pairs)  10.6 us
    another operation x1, loops' own time, on_device(): lax.fori_loop(0, members - 1, relay, (nothing, local_add))  9.8 us
    convert_element_type x6, local copies, waits for them, and re-layouts, heads_first(): return jnp.transpose(array.reshape(blocks, BLOCK, group_total, GROUP_DIME...  9.15 us
    dot_general x5, matrix products, contract_score(): return jnp.einsum(form, left_side, right_side, precision=SCORE_PRECISION)  8.73 us
  transfers between devices with their start and end apart: 4, of which 4 were waited for; matrix products, arithmetic and copies ran while one was open for 4% of the time, Pallas kernels for 0%

commit v1 on v0

v1 whole, which is shorter than its diff:
```python
import functools

import jax
import jax.numpy as jnp
from jax import lax
from jax.experimental import pallas as pl
from jax.experimental.pallas import tpu as pltpu
from jax.sharding import PartitionSpec as P

C = 64
LANES = 128
KEY_EPS = 1e-05
NORM_EPS = 0.00064
FINE_LEVELS = 4
GROUP = 2
F32 = jnp.float32
BF16 = jnp.bfloat16
MESH = pl.DeviceIdType.MESH


def split(x):
    hi = x.astype(BF16)
    return hi, (x - hi.astype(F32)).astype(BF16)


def dot(a, b):
    return lax.dot_general(a, b, (((1,), (0,)), ((), ())), preferred_element_type=F32)


def dot_t(a, b):
    return lax.dot_general(a, b, (((1,), (1,)), ((), ())), preferred_element_type=F32)


def cat(parts, axis):
    return jnp.concatenate(parts, axis)


def lane_ids(rows):
    return lax.broadcasted_iota(jnp.int32, (rows, LANES), 1)


def head_sum(x, ones2):
    hi, lo = split(x)
    return dot(cat([hi, lo], 1), ones2)


def head_ones():
    rows = lax.broadcasted_iota(jnp.int32, (2 * LANES, LANES), 0)
    cols = lax.broadcasted_iota(jnp.int32, (2 * LANES, LANES), 1)
    same = lax.rem(rows, LANES) // C == cols // C
    return jnp.where(same, 1.0, 0.0).astype(BF16)


def diagonal_state(z):
    first = lane_ids(C) < C
    return cat([jnp.where(first, z, 0.0), jnp.where(first, 0.0, z)], 0)


def product3(a, b):
    ahi, alo = split(a)
    bhi, blo = split(b)
    return dot(cat([ahi, alo], 1), cat([bhi, bhi], 0)) + dot(ahi, blo)


def kernel(
    members,
    r_ref, lf_ref, k_ref, v_ref, e_ref, a_ref, u_ref, g_ref,
    out_ref, final_ref,
    w_buf, add_buf, z_in, z_out, s_buf,
    send_sem, recv_sem, fsend_sem, frecv_sem, local_sem,
):
    T, channels = r_ref.shape
    pairs = channels // LANES
    groups = pairs // GROUP
    share = final_ref.shape[0]
    last = members - 1
    me = lax.axis_index("seq")
    barrier = pltpu.get_barrier_semaphore()
    for hop in range(1, members):
        pl.semaphore_signal(
            barrier, inc=1, device_id={"seq": lax.rem(me + hop, members)}, device_id_type=MESH
        )
    pl.semaphore_wait(barrier, members - 1)

    @pl.when(me == 0)
    def _():
        z_in[...] = jnp.zeros_like(z_in)

    def lanes_of(pair):
        return pl.ds(pl.multiple_of(pair * LANES, LANES), LANES)

    def compute(group):
        rows = lax.broadcasted_iota(jnp.int32, (T, T), 0)
        cols = lax.broadcasted_iota(jnp.int32, (T, T), 1)
        inclusive = rows >= cols
        strict = rows > cols
        lower = jnp.where(inclusive, 1.0, 0.0).astype(BF16)
        first = lane_ids(T) < C
        ones2 = head_ones()
        state_lanes = lane_ids(T + C) < C
        diag = lax.rem(lane_ids(C), C) == lax.broadcasted_iota(jnp.int32, (C, LANES), 0)
        heads = []
        ends = []
        for j in range(GROUP):
            at = lanes_of(group * GROUP + j)
            w = -jnp.exp(lf_ref[:, at].astype(F32))
            whi, wlo = split(w)
            both = dot(lower, cat([whi, wlo], 1))
            cum = both[:, :LANES] + both[:, LANES:]
            mid = cum[T // 2 - 1 : T // 2, :]
            end = cum[T - 1 : T, :]
            c = cum - mid
            e_c = jnp.exp(c)
            e_b = jnp.exp(c - w)
            e_inv = jnp.exp(-c)
            g_mid = jnp.exp(mid)
            g_end = jnp.exp(end - mid)
            gamma = jnp.exp(end)
            e = e_ref[:, at].astype(F32)
            kappa = e * lax.rsqrt(head_sum(e * e, ones2) * (1.0 / C) + KEY_EPS) * C**-0.5
            toward = -kappa * e_b
            reader = r_ref[:, at].astype(F32) * e_c
            away = kappa * a_ref[:, at].astype(F32) * e_inv
            keys = k_ref[:, at].astype(F32) * e_inv
            toward_true = toward * g_mid
            reader_true = reader * g_mid
            away_t = jnp.transpose(away * g_end)
            keys_t = jnp.transpose(keys * g_end)
            vroll = pltpu.roll(v_ref[:, at].astype(F32), C, 1)
            vroll_b = vroll.astype(BF16)
            vroll2 = cat([vroll_b, vroll_b], 0)
            qhi, qlo = split(cat([toward, reader], 0))
            q2 = cat([qhi, qlo], 1)
            ends.append((reader_true, jnp.where(diag, gamma, 0.0)))
            for h in range(2):
                own = first if h == 0 else jnp.logical_not(first)
                sides = cat([jnp.where(own, away, 0.0), jnp.where(own, keys, 0.0)], 0)
                khi, klo = split(sides)
                scores = dot_t(q2, cat([khi, khi], 1)) + dot_t(qhi, klo)
                mix_away = jnp.where(strict, scores[:T, :T], 0.0)
                mix_keys = jnp.where(strict, scores[:T, T:], 0.0)
                read = cat(
                    [
                        jnp.where(inclusive, scores[T:, :T], 0.0),
                        jnp.where(inclusive, scores[T:, T:], 0.0),
                    ],
                    1,
                )
                closing = cat([away_t[h * C : h * C + C], keys_t[h * C : h * C + C]], 1)
                mhi, mlo = split(mix_keys)
                mixed = dot(cat([mhi, mlo], 1), vroll2)
                heads.append(
                    dict(
                        y=mix_away,
                        x=jnp.where(own, toward_true, mixed),
                        left=cat([read, closing], 0),
                        v=jnp.where(own, 0.0, vroll).astype(BF16),
                    )
                )
        levels = (T - 1).bit_length()
        for level in range(levels):
            fine = level < FINE_LEVELS
            for head in heads:
                y, x = head["y"], head["x"]
                right = x if level == levels - 1 else cat([y, x], 1)
                if fine:
                    yhi, ylo = split(y)
                    rhi, rlo = split(right)
                    prod = dot(cat([yhi, ylo], 1), cat([rhi, rhi], 0)) + dot(yhi, rlo)
                else:
                    prod = dot(y.astype(BF16), right.astype(BF16))
                head["y"] = prod[:, :T]
                head["x"] = x + prod[:, -LANES:]
        for j in range(GROUP):
            results = []
            for head in heads[2 * j : 2 * j + 2]:
                lhi, llo = split(head["left"])
                xhi, xlo = split(head["x"])
                rhi = cat([xhi, head["v"]], 0)
                results.append(dot(lhi, rhi) + dot(llo, rhi) + dot(lhi[:, :T], xlo))
            pair = group * GROUP + j
            w_buf[pair] = jnp.where(state_lanes, results[0], results[1]) + cat(list(ends[j]), 0)
            add_buf[pair] = pltpu.roll(jnp.where(state_lanes, results[1], results[0]), C, 1)

    def state_copy(pair):
        return pltpu.make_async_remote_copy(
            src_ref=z_out.at[pair],
            dst_ref=z_in.at[pair],
            send_sem=send_sem.at[pair],
            recv_sem=recv_sem.at[pair],
            device_id={"seq": lax.rem(me + 1, members)},
            device_id_type=MESH,
        )

    def relay(group):
        for j in range(GROUP):
            pair = group * GROUP + j

            @pl.when(me > 0)
            def _():
                state_copy(pair).wait_recv()

            z = diagonal_state(z_in[pair])
            leaving = product3(w_buf[pair, T:, :], z) + add_buf[pair, T:, :]
            z_out[pair] = leaving

            @pl.when(me < last)
            def _():
                state_copy(pair).start()

            @pl.when(me == last)
            def _():
                s_buf[pl.ds(pl.multiple_of(pair * LANES, LANES), LANES), :] = jnp.transpose(leaving)

    def finish(group):
        ones2 = head_ones()
        for j in range(GROUP):
            pair = group * GROUP + j
            at = lanes_of(pair)
            z = diagonal_state(z_in[pair])
            result = product3(w_buf[pair, :T, :], z) + add_buf[pair, :T, :]
            average = head_sum(result, ones2) * (1.0 / C)
            centered = result - average
            spread = head_sum(centered * centered, ones2) * (1.0 / C)
            normed = centered * lax.rsqrt(spread + NORM_EPS) * g_ref[:, at]
            bonus = r_ref[:, at].astype(F32) * k_ref[:, at].astype(F32) * u_ref[:, at]
            extra = head_sum(bonus, ones2) * v_ref[:, at].astype(F32)
            out_ref[:, at] = (normed + extra).astype(out_ref.dtype)

    def step(s, _):
        @pl.when(s < groups)
        def _():
            compute(s)

        @pl.when(jnp.logical_and(s >= me, s - me < groups))
        def _():
            relay(s - me)

        return 0

    lax.fori_loop(0, groups + members - 1, step, 0)

    def final_copy(target):
        return pltpu.make_async_remote_copy(
            src_ref=s_buf.at[pl.ds(pl.multiple_of(target * share, 8), share), :],
            dst_ref=final_ref,
            send_sem=fsend_sem.at[target],
            recv_sem=frecv_sem,
            device_id={"seq": target},
            device_id_type=MESH,
        )

    @pl.when(me == last)
    def _():
        for target in range(last):
            final_copy(target).start()
        own = pltpu.make_async_copy(
            s_buf.at[pl.ds(last * share, share), :], final_ref, local_sem
        )
        own.start()
        own.wait()

    def finish_step(s, _):
        finish(s)
        return 0

    lax.fori_loop(0, groups, finish_step, 0)

    @pl.when(me == last)
    def _():
        for target in range(last):
            final_copy(target).wait_send()

    @pl.when(me < last)
    def _():
        final_copy(0).wait_recv()

        def sent(pair, _):
            state_copy(pair).wait_send()
            return 0

        lax.fori_loop(0, pairs, sent, 0)


def on_device(r, lf, k, v, e, a, u, g, *, members):
    sequences, T, channels = r.shape
    pairs = channels // LANES
    share = channels // members
    call = pl.pallas_call(
        functools.partial(kernel, members),
        out_shape=(
            jax.ShapeDtypeStruct((T, channels), BF16),
            jax.ShapeDtypeStruct((share, C), F32),
        ),
        in_specs=[pl.BlockSpec(memory_space=pltpu.VMEM)] * 8,
        out_specs=[pl.BlockSpec(memory_space=pltpu.VMEM)] * 2,
        scratch_shapes=[
            pltpu.VMEM((pairs, T + C, LANES), F32),
            pltpu.VMEM((pairs, T + C, LANES), F32),
            pltpu.VMEM((pairs, C, LANES), F32),
            pltpu.VMEM((pairs, C, LANES), F32),
            pltpu.VMEM((channels, C), F32),
            pltpu.SemaphoreType.DMA((pairs,)),
            pltpu.SemaphoreType.DMA((pairs,)),
            pltpu.SemaphoreType.DMA((members - 1,)),
            pltpu.SemaphoreType.DMA,
            pltpu.SemaphoreType.DMA,
        ],
        compiler_params=pltpu.CompilerParams(
            collective_id=0, has_side_effects=True, vmem_limit_bytes=48 * 1024 * 1024
        ),
    )
    out, final = call(
        *(x.reshape(T, channels) for x in (r, lf, k, v, e, a)),
        u.reshape(1, channels),
        g.reshape(1, channels),
    )
    return out.reshape(sequences, T, channels), final.reshape(sequences, share, C)


def solution(mesh):
    split_spec = P(("groups", "dp"), "seq", None)
    return jax.shard_map(
        functools.partial(on_device, members=mesh.shape["seq"]),
        mesh=mesh,
        in_specs=(split_spec,) * 6 + (P(), P()),
        out_specs=(split_spec, split_spec),
        check_vma=False,
    )
```

time: 389 us -> 47.9 us (0.12); the launches traced: 383 us -> 47.5 us
  other arithmetic: 209 us -> 0 us
  waiting for transfers between devices: 62.2 us -> 0 us
  matrix products: 43.5 us -> 0 us
  Pallas kernels: 0 us -> 38.8 us
  local copies, waits for them, and re-layouts: 32.7 us -> 8.01 us
  between operations: 14.8 us -> 0.67 us
  starting transfers between devices: 10.6 us -> 0 us
  loops' own time: 9.93 us -> 0 us
    another operation x8 -> x0, other arithmetic: 201 us -> none  [the longest x4 200 us: local_pass(): lax.linalg.triangular_solve(system, known_side, left_side=True, lower=Tru...]
    ppermute x3 -> x0, waiting for transfers between devices: 42 us -> none  [passed_along(): return lax.ppermute(shard, axis, pairs)]
    pallas_call x0 -> x1, Pallas kernels: none -> 38.8 us  [on_device(): call(*(x.reshape(T, channels) for x in (r, lf, k, v, e, a)), u.reshape(1,...]
    dot_general x18 -> x0, matrix products: 36.5 us -> none  [the longest x13 27.7 us: contract(): return jnp.einsum(form, left_side, right_side, precision=HIGHEST_PRECISION)]
    psum x1 -> x0, waiting for transfers between devices: 20.3 us -> none  [broadcast(): return lax.psum(kept, axis)]
    ppermute x3 -> x0, starting transfers between devices: 10.6 us -> none  [passed_along(): return lax.ppermute(shard, axis, pairs)]
    another operation x2 -> x0, loops' own time: 9.93 us -> none  [the longest x1 9.8 us: on_device(): lax.fori_loop(0, members - 1, relay, (nothing, local_add))]
    convert_element_type x7 -> x0, local copies, waits for them, and re-layouts: 9.22 us -> none  [the longest x6 9.15 us: heads_first(): return jnp.transpose(array.reshape(blocks, BLOCK, group_total, GROUP_DIME...]
  transfers between devices with their start and end apart: 4 -> 0, of which waited for: 4 -> 0; matrix products, arithmetic and copies ran while one was open for 4% -> 0% of each run, Pallas kernels for 0% -> 0%
where the time goes in v1:
time: 47.9 us; the launch traced here: 47.5 us
  Pallas kernels  38.8 us (81%)
  local copies, waits for them, and re-layouts  8.01 us (17%)
  between operations  0.67 us (1%)
    pallas_call x1, Pallas kernels, on_device(): call(*(x.reshape(T, channels) for x in (r, lf, k, v, e, a)), u.reshape(1,...  38.8 us
    unnamed x18, local copies, waits for them, and re-layouts  8 us

profile of v1, /device:TPU:18, one launch (start us, length us, event | category | flops | bytes accessed | tf_op | source)
XLA Modules:
  0.0 47.5 jit_solution(3670144488330351824)
XLA Ops:
  0.6 0.0 copy-start.6
  0.6 0.0 copy-start.7
  0.6 0.7 %copy-done.6 = f32[1280]{0:T(1024)S(1)} copy-done((f32[1280]{0:T(1024)S(1)}, f32[1280]{0:T(1024)}, u32[]{:S(2)}) %copy-start.6) | copy-done | bytes 5144
  1.3 0.0 copy-done.7
  1.3 0.0 copy-start
  1.4 1.0 %copy-done = bf16[1,128,1280]{2,1,0:T(8,128)(2,1)S(1)} copy-done((bf16[1,128,1280]{2,1,0:T(8,128)(2,1)S(1)}, bf16[1,128,1280]{2,1,0:T(8,128)(2,1)}, u32[]{:S(2)}) %copy-start) | copy-done | bytes 327704
  2.3 0.0 copy-start.1
  2.3 1.0 %copy-done.1 = bf16[1,128,1280]{2,1,0:T(8,128)(2,1)S(1)} copy-done((bf16[1,128,1280]{2,1,0:T(8,128)(2,1)S(1)}, bf16[1,128,1280]{2,1,0:T(8,128)(2,1)}, u32[]{:S(2)}) %copy-start.1) | copy-done | bytes 327704
  3.3 0.0 copy-start.2
  3.3 1.0 %copy-done.2 = bf16[1,128,1280]{2,1,0:T(8,128)(2,1)S(1)} copy-done((bf16[1,128,1280]{2,1,0:T(8,128)(2,1)S(1)}, bf16[1,128,1280]{2,1,0:T(8,128)(2,1)}, u32[]{:S(2)}) %copy-start.2) | copy-done | bytes 327704
  4.3 0.0 copy-start.3
  4.3 1.0 %copy-done.3 = bf16[1,128,1280]{2,1,0:T(8,128)(2,1)S(1)} copy-done((bf16[1,128,1280]{2,1,0:T(8,128)(2,1)S(1)}, bf16[1,128,1280]{2,1,0:T(8,128)(2,1)}, u32[]{:S(2)}) %copy-start.3) | copy-done | bytes 327704
  5.2 0.0 copy-start.4
  5.2 1.0 %copy-done.4 = bf16[1,128,1280]{2,1,0:T(8,128)(2,1)S(1)} copy-done((bf16[1,128,1280]{2,1,0:T(8,128)(2,1)S(1)}, bf16[1,128,1280]{2,1,0:T(8,128)(2,1)}, u32[]{:S(2)}) %copy-start.4) | copy-done | bytes 327704
  6.2 0.0 copy-start.5
  6.2 1.0 %copy-done.5 = bf16[1,128,1280]{2,1,0:T(8,128)(2,1)S(1)} copy-done((bf16[1,128,1280]{2,1,0:T(8,128)(2,1)S(1)}, bf16[1,128,1280]{2,1,0:T(8,128)(2,1)}, u32[]{:S(2)}) %copy-start.5) | copy-done | bytes 327704
  7.2 38.8 %shard_map.95 = (bf16[128,1280]{1,0:T(8,128)(2,1)S(1)}, f32[320,64]{1,0:T(8,128)S(1)}) custom-call(bf16[128,1280]{1,0:T(8,128)(2,1)S(1)} %bitcast.9, bf16[128,1280]{1,0:T(8,128)(2,1)S(1)} %bitcast.10, bf16[128,1280]{1,0:T(8,128)(2,1)S(1)} %bitcast.11, bf16[128,1280]{1,0:T(8,128)(2,1)S(1)} %bitcast.12, bf16[128,1280]{1,0:T(8,128)(2,1)S(1)} %bitcast.13, ...), custom_call_target="tpu_custom_call" | custom-call | tf_op jit(solution)/shard_map/pallas_call | solution.py:313
  46.0 0.8 %copy.10 = f32[1,320,64]{1,2,0:T(8,128)} copy(f32[1,320,64]{2,1,0:T(8,128)S(1)} %bitcast.15) | data formatting | bytes 163840
  46.8 0.7 %copy.12 = bf16[1,128,1280]{2,1,0:T(8,128)(2,1)} copy(bf16[1,128,1280]{2,1,0:T(8,128)(2,1)S(1)} %bitcast.8) | data formatting | bytes 655360
  (2 shorter events, 0.0 us)
Async XLA Ops:
  0.6 0.7 %copy-start.6 = (f32[1280]{0:T(1024)S(1)}, f32[1280]{0:T(1024)}, u32[]{:S(2)}) copy-start(f32[1280]{0:T(1024)} %param.14) | copy-start | bytes 15364
  0.6 0.7 %copy-start.7 = (f32[1280]{0:T(1024)S(1)}, f32[1280]{0:T(1024)}, u32[]{:S(2)}) copy-start(f32[1280]{0:T(1024)} %param.15) | copy-start | bytes 15364
  1.3 1.0 %copy-start = (bf16[1,128,1280]{2,1,0:T(8,128)(2,1)S(1)}, bf16[1,128,1280]{2,1,0:T(8,128)(2,1)}, u32[]{:S(2)}) copy-start(bf16[1,128,1280]{2,1,0:T(8,128)(2,1)} %param.8) | copy-start | bytes 983044
  2.3 1.0 %copy-start.1 = (bf16[1,128,1280]{2,1,0:T(8,128)(2,1)S(1)}, bf16[1,128,1280]{2,1,0:T(8,128)(2,1)}, u32[]{:S(2)}) copy-start(bf16[1,128,1280]{2,1,0:T(8,128)(2,1)} %param.9) | copy-start | bytes 983044
  3.3 1.0 %copy-start.2 = (bf16[1,128,1280]{2,1,0:T(8,128)(2,1)S(1)}, bf16[1,128,1280]{2,1,0:T(8,128)(2,1)}, u32[]{:S(2)}) copy-start(bf16[1,128,1280]{2,1,0:T(8,128)(2,1)} %param.10) | copy-start | bytes 983044
  4.3 1.0 %copy-start.3 = (bf16[1,128,1280]{2,1,0:T(8,128)(2,1)S(1)}, bf16[1,128,1280]{2,1,0:T(8,128)(2,1)}, u32[]{:S(2)}) copy-start(bf16[1,128,1280]{2,1,0:T(8,128)(2,1)} %param.11) | copy-start | bytes 983044
  5.2 1.0 %copy-start.4 = (bf16[1,128,1280]{2,1,0:T(8,128)(2,1)S(1)}, bf16[1,128,1280]{2,1,0:T(8,128)(2,1)}, u32[]{:S(2)}) copy-start(bf16[1,128,1280]{2,1,0:T(8,128)(2,1)} %param.12) | copy-start | bytes 983044
  6.2 1.0 %copy-start.5 = (bf16[1,128,1280]{2,1,0:T(8,128)(2,1)S(1)}, bf16[1,128,1280]{2,1,0:T(8,128)(2,1)}, u32[]{:S(2)}) copy-start(bf16[1,128,1280]{2,1,0:T(8,128)(2,1)} %param.13) | copy-start | bytes 983044

commit v2 on v1

--- a/solution.py
+++ b/solution.py
@@ -11,7 +11,7 @@
 LANES = 128
 KEY_EPS = 1e-05
 NORM_EPS = 0.00064
-FINE_LEVELS = 4
+FINE_LEVELS = 3
 GROUP = 2
 F32 = jnp.float32
 BF16 = jnp.bfloat16
@@ -59,15 +59,16 @@
 def product3(a, b):
     ahi, alo = split(a)
     bhi, blo = split(b)
-    return dot(cat([ahi, alo], 1), cat([bhi, bhi], 0)) + dot(ahi, blo)
+    return dot(cat([ahi, alo, ahi], 1), cat([bhi, bhi, blo], 0))
 
 
 def kernel(
     members,
+    r_in, lf_in, k_in, v_in, e_in, a_in, u_in, g_in,
+    out_ref, final_ref,
     r_ref, lf_ref, k_ref, v_ref, e_ref, a_ref, u_ref, g_ref,
-    out_ref, final_ref,
     w_buf, add_buf, z_in, z_out, s_buf,
-    send_sem, recv_sem, fsend_sem, frecv_sem, local_sem,
+    send_sem, recv_sem, fsend_sem, frecv_sem, local_sem, in_sem, gain_sem,
 ):
     T, channels = r_ref.shape
     pairs = channels // LANES
@@ -80,7 +81,28 @@
         pl.semaphore_signal(
             barrier, inc=1, device_id={"seq": lax.rem(me + hop, members)}, device_id_type=MESH
         )
-    pl.semaphore_wait(barrier, members - 1)
+
+    arrays = (
+        (r_in, r_ref), (lf_in, lf_ref), (k_in, k_ref), (v_in, v_ref), (e_in, e_ref), (a_in, a_ref)
+    )
+    gains = ((u_in, u_ref), (g_in, g_ref))
+
+    def input_copies(group):
+        at = pl.ds(pl.multiple_of(group * (GROUP * LANES), LANES), GROUP * LANES)
+        return [
+            pltpu.make_async_copy(source.at[:, at], target.at[:, at], in_sem.at[i, group])
+            for i, (source, target) in enumerate(arrays)
+        ]
+
+    for group in range(groups):
+        for copy in input_copies(group):
+            copy.start()
+    gain_copies = [
+        pltpu.make_async_copy(source, target, gain_sem.at[i])
+        for i, (source, target) in enumerate(gains)
+    ]
+    for copy in gain_copies:
+        copy.start()
 
     @pl.when(me == 0)
     def _():
@@ -90,6 +112,8 @@
         return pl.ds(pl.multiple_of(pair * LANES, LANES), LANES)
 
     def compute(group):
+        for copy in input_copies(group):
+            copy.wait()
         rows = lax.broadcasted_iota(jnp.int32, (T, T), 0)
         cols = lax.broadcasted_iota(jnp.int32, (T, T), 1)
         inclusive = rows >= cols
@@ -130,13 +154,13 @@
             vroll_b = vroll.astype(BF16)
             vroll2 = cat([vroll_b, vroll_b], 0)
             qhi, qlo = split(cat([toward, reader], 0))
-            q2 = cat([qhi, qlo], 1)
+            q3 = cat([qhi, qlo, qhi], 1)
             ends.append((reader_true, jnp.where(diag, gamma, 0.0)))
             for h in range(2):
                 own = first if h == 0 else jnp.logical_not(first)
                 sides = cat([jnp.where(own, away, 0.0), jnp.where(own, keys, 0.0)], 0)
                 khi, klo = split(sides)
-                scores = dot_t(q2, cat([khi, khi], 1)) + dot_t(qhi, klo)
+                scores = dot_t(q3, cat([khi, khi, klo], 1))
                 mix_away = jnp.where(strict, scores[:T, :T], 0.0)
                 mix_keys = jnp.where(strict, scores[:T, T:], 0.0)
                 read = cat(
@@ -166,7 +190,7 @@
                 if fine:
                     yhi, ylo = split(y)
                     rhi, rlo = split(right)
-                    prod = dot(cat([yhi, ylo], 1), cat([rhi, rhi], 0)) + dot(yhi, rlo)
+                    prod = dot(cat([yhi, ylo, yhi], 1), cat([rhi, rhi, rlo], 0))
                 else:
                     prod = dot(y.astype(BF16), right.astype(BF16))
                 head["y"] = prod[:, :T]
@@ -177,7 +201,7 @@
                 lhi, llo = split(head["left"])
                 xhi, xlo = split(head["x"])
                 rhi = cat([xhi, head["v"]], 0)
-                results.append(dot(lhi, rhi) + dot(llo, rhi) + dot(lhi[:, :T], xlo))
+                results.append(dot(cat([lhi, llo, lhi[:, :T]], 1), cat([rhi, rhi, xlo], 0)))
             pair = group * GROUP + j
             w_buf[pair] = jnp.where(state_lanes, results[0], results[1]) + cat(list(ends[j]), 0)
             add_buf[pair] = pltpu.roll(jnp.where(state_lanes, results[1], results[0]), C, 1)
@@ -227,19 +251,6 @@
             extra = head_sum(bonus, ones2) * v_ref[:, at].astype(F32)
             out_ref[:, at] = (normed + extra).astype(out_ref.dtype)
 
-    def step(s, _):
-        @pl.when(s < groups)
-        def _():
-            compute(s)
-
-        @pl.when(jnp.logical_and(s >= me, s - me < groups))
-        def _():
-            relay(s - me)
-
-        return 0
-
-    lax.fori_loop(0, groups + members - 1, step, 0)
-
     def final_copy(target):
         return pltpu.make_async_remote_copy(
             src_ref=s_buf.at[pl.ds(pl.multiple_of(target * share, 8), share), :],
@@ -250,24 +261,55 @@
             device_id_type=MESH,
         )
 
+    def own_copy():
+        return pltpu.make_async_copy(s_buf.at[pl.ds(last * share, share), :], final_ref, local_sem)
+
+    group_rows = GROUP * LANES
+    finish_from = jnp.maximum(me + 1, groups - (me // last) * groups)
+
+    def step(s, _):
+        @pl.when(s < groups)
+        def _():
+            compute(s)
+
+        @pl.when(s == 0)
+        def _():
+            pl.semaphore_wait(barrier, members - 1)
+            for copy in gain_copies:
+                copy.wait()
+
+        done = s - finish_from
+
+        @pl.when(jnp.logical_and(done >= 0, done < groups))
+        def _():
+            finish(done)
+
+        turn = s - me
+
+        @pl.when(jnp.logical_and(turn >= 0, turn < groups))
+        def _():
+            relay(turn)
+
+            @pl.when(me == last)
+            def _():
+                for target in range(last):
+                    ready = -(-(target + 1) * share // group_rows) - 1
+
+                    @pl.when(turn == ready)
+                    def _():
+                        final_copy(target).start()
+
+                @pl.when(turn == groups - 1)
+                def _():
+                    own_copy().start()
+
+        return 0
+
+    lax.fori_loop(0, groups + max(groups, members), step, 0)
+
     @pl.when(me == last)
     def _():
-        for target in range(last):
-            final_copy(target).start()
-        own = pltpu.make_async_copy(
-            s_buf.at[pl.ds(last * share, share), :], final_ref, local_sem
-        )
-        own.start()
-        own.wait()
-
-    def finish_step(s, _):
-        finish(s)
-        return 0
-
-    lax.fori_loop(0, groups, finish_step, 0)
-
-    @pl.when(me == last)
-    def _():
+        own_copy().wait()
         for target in range(last):
             final_copy(target).wait_send()
 
@@ -292,9 +334,11 @@
             jax.ShapeDtypeStruct((T, channels), BF16),
             jax.ShapeDtypeStruct((share, C), F32),
         ),
-        in_specs=[pl.BlockSpec(memory_space=pltpu.VMEM)] * 8,
+        in_specs=[pl.BlockSpec(memory_space=pl.ANY)] * 8,
         out_specs=[pl.BlockSpec(memory_space=pltpu.VMEM)] * 2,
-        scratch_shapes=[
+        scratch_shapes=[pltpu.VMEM((T, channels), BF16)] * 6
+        + [pltpu.VMEM((1, channels), F32)] * 2
+        + [
             pltpu.VMEM((pairs, T + C, LANES), F32),
             pltpu.VMEM((pairs, T + C, LANES), F32),
             pltpu.VMEM((pairs, C, LANES), F32),
@@ -305,9 +349,11 @@
             pltpu.SemaphoreType.DMA((members - 1,)),
             pltpu.SemaphoreType.DMA,
             pltpu.SemaphoreType.DMA,
+            pltpu.SemaphoreType.DMA((6, pairs // GROUP)),
+            pltpu.SemaphoreType.DMA((2,)),
         ],
         compiler_params=pltpu.CompilerParams(
-            collective_id=0, has_side_effects=True, vmem_limit_bytes=48 * 1024 * 1024
+            collective_id=0, has_side_effects=True, vmem_limit_bytes=60 * 1024 * 1024
         ),
     )
     out, final = call(

time: 47.9 us -> 39 us (0.81)
  Pallas kernels: 38.8 us -> 32.8 us
  local copies, waits for them, and re-layouts: 8.01 us -> 5.27 us
    pallas_call x1, Pallas kernels: 38.8 us -> 32.8 us  [on_device(): call(*(x.reshape(T, channels) for x in (r, lf, k, v, e, a)), u.reshape(1,...]
    unnamed x18 -> x6, local copies, waits for them, and re-layouts: 8 us -> 4.07 us
    reshape x1, local copies, waits for them, and re-layouts: 0.01 us -> 0.6 us  [on_device(): g.reshape(1, channels)]
    reshape x1, local copies, waits for them, and re-layouts: 0.01 us -> 0.6 us  [on_device(): u.reshape(1, channels)]
where the time goes in v2:
time: 39 us; the launch traced here: 38.7 us
  Pallas kernels  32.8 us (84%)
  local copies, waits for them, and re-layouts  5.27 us (14%)
  between operations  0.66 us (2%)
    pallas_call x1, Pallas kernels, on_device(): call(*(x.reshape(T, channels) for x in (r, lf, k, v, e, a)), u.reshape(1,...  32.8 us
    unnamed x6, local copies, waits for them, and re-layouts  4.07 us

profile of v2, /device:TPU:18, one launch (start us, length us, event | category | flops | bytes accessed | tf_op | source)
XLA Modules:
  0.0 38.7 jit_solution(15429183018170933843)
XLA Ops:
  0.6 0.0 copy-start
  0.6 0.0 copy-start.1
  0.6 0.7 %copy-done = f32[1280]{0:T(1024)S(1)} copy-done((f32[1280]{0:T(1024)S(1)}, f32[1280]{0:T(1024)}, u32[]{:S(2)}) %copy-start) | copy-done | bytes 5144
  1.3 0.6 %reshape.40.u_in = f32[1,1280]{1,0:T(1,128)} reshape(f32[1280]{0:T(1024)S(1)} %copy-done) | data formatting | bytes 10240 | tf_op jit(solution)/shard_map/reshape | solution.py:361
  1.9 0.0 copy-done.1
  1.9 0.6 %reshape.41.g_in = f32[1,1280]{1,0:T(1,128)} reshape(f32[1280]{0:T(1024)S(1)} %copy-done.1) | data formatting | bytes 10240 | tf_op jit(solution)/shard_map/reshape | solution.py:362
  2.5 32.8 %shard_map.95 = (bf16[128,1280]{1,0:T(8,128)(2,1)}, f32[320,64]{1,0:T(8,128)}) custom-call(bf16[128,1280]{1,0:T(8,128)(2,1)} %bitcast.9, bf16[128,1280]{1,0:T(8,128)(2,1)} %bitcast.10, bf16[128,1280]{1,0:T(8,128)(2,1)} %bitcast.11, bf16[128,1280]{1,0:T(8,128)(2,1)} %bitcast.12, bf16[128,1280]{1,0:T(8,128)(2,1)} %bitcast.13, bf16[128,1280]{1,0:T(8,128)(2,1)} %bitcast.14, ...), custom_call_target="tpu_custom_call" | custom-call | tf_op jit(solution)/shard_map/pallas_call | solution.py:359
  35.3 1.7 %copy.10 = f32[1,320,64]{1,2,0:T(8,128)} copy(f32[1,320,64]{2,1,0:T(8,128)} %bitcast.15) | data formatting | bytes 163840
  37.0 1.7 %copy.12 = bf16[1,128,1280]{2,1,0:T(8,128)(2,1)} copy(bf16[1,128,1280]{2,1,0:T(8,128)(2,1)} %bitcast.8) | data formatting | bytes 655360
Async XLA Ops:
  0.6 0.7 %copy-start = (f32[1280]{0:T(1024)S(1)}, f32[1280]{0:T(1024)}, u32[]{:S(2)}) copy-start(f32[1280]{0:T(1024)} %param.14) | copy-start | bytes 15364
  0.6 1.3 %copy-start.1 = (f32[1280]{0:T(1024)S(1)}, f32[1280]{0:T(1024)}, u32[]{:S(2)}) copy-start(f32[1280]{0:T(1024)} %param.15) | copy-start | bytes 15364

commit v3 on v2

--- a/solution.py
+++ b/solution.py
@@ -12,7 +12,7 @@
 KEY_EPS = 1e-05
 NORM_EPS = 0.00064
 FINE_LEVELS = 3
-GROUP = 2
+GROUP = 5
 F32 = jnp.float32
 BF16 = jnp.bfloat16
 MESH = pl.DeviceIdType.MESH
@@ -64,11 +64,11 @@
 
 def kernel(
     members,
-    r_in, lf_in, k_in, v_in, e_in, a_in, u_in, g_in,
+    r_in, lf_in, k_in, v_in, e_in, a_in, u_ref, g_ref,
     out_ref, final_ref,
-    r_ref, lf_ref, k_ref, v_ref, e_ref, a_ref, u_ref, g_ref,
+    r_ref, lf_ref, k_ref, v_ref, e_ref, a_ref,
     w_buf, add_buf, z_in, z_out, s_buf,
-    send_sem, recv_sem, fsend_sem, frecv_sem, local_sem, in_sem, gain_sem,
+    send_sem, recv_sem, fsend_sem, frecv_sem, local_sem, in_sem,
 ):
     T, channels = r_ref.shape
     pairs = channels // LANES
@@ -85,7 +85,6 @@
     arrays = (
         (r_in, r_ref), (lf_in, lf_ref), (k_in, k_ref), (v_in, v_ref), (e_in, e_ref), (a_in, a_ref)
     )
-    gains = ((u_in, u_ref), (g_in, g_ref))
 
     def input_copies(group):
         at = pl.ds(pl.multiple_of(group * (GROUP * LANES), LANES), GROUP * LANES)
@@ -97,12 +96,6 @@
     for group in range(groups):
         for copy in input_copies(group):
             copy.start()
-    gain_copies = [
-        pltpu.make_async_copy(source, target, gain_sem.at[i])
-        for i, (source, target) in enumerate(gains)
-    ]
-    for copy in gain_copies:
-        copy.start()
 
     @pl.when(me == 0)
     def _():
@@ -184,17 +177,24 @@
         levels = (T - 1).bit_length()
         for level in range(levels):
             fine = level < FINE_LEVELS
+            skip = 2**level if 2**level >= 16 else 0
+            later = 2 ** (level + 1) if 2 ** (level + 1) >= 16 else 0
             for head in heads:
                 y, x = head["y"], head["x"]
-                right = x if level == levels - 1 else cat([y, x], 1)
                 if fine:
                     yhi, ylo = split(y)
-                    rhi, rlo = split(right)
+                    rhi, rlo = split(cat([y, x], 1))
                     prod = dot(cat([yhi, ylo, yhi], 1), cat([rhi, rhi, rlo], 0))
                 else:
-                    prod = dot(y.astype(BF16), right.astype(BF16))
-                head["y"] = prod[:, :T]
-                head["x"] = x + prod[:, -LANES:]
+                    y, right = y.astype(BF16), x.astype(BF16)
+                    if level < levels - 1:
+                        full = cat([jnp.zeros((skip, T), BF16), y], 0) if skip else y
+                        right = cat([full, right], 1)
+                    prod = dot(y, right)
+                if level < levels - 1:
+                    head["y"] = prod[later - skip :, :T]
+                gained = prod[:, -LANES:]
+                head["x"] = cat([x[:skip], x[skip:] + gained], 0) if skip else x + gained
         for j in range(GROUP):
             results = []
             for head in heads[2 * j : 2 * j + 2]:
@@ -220,13 +220,15 @@
         for j in range(GROUP):
             pair = group * GROUP + j
 
+            @pl.when(me == 0)
+            def _():
+                z_out[pair] = add_buf[pair, T:, :]
+
             @pl.when(me > 0)
             def _():
                 state_copy(pair).wait_recv()
-
-            z = diagonal_state(z_in[pair])
-            leaving = product3(w_buf[pair, T:, :], z) + add_buf[pair, T:, :]
-            z_out[pair] = leaving
+                z = diagonal_state(z_in[pair])
+                z_out[pair] = product3(w_buf[pair, T:, :], z) + add_buf[pair, T:, :]
 
             @pl.when(me < last)
             def _():
@@ -234,7 +236,9 @@
 
             @pl.when(me == last)
             def _():
-                s_buf[pl.ds(pl.multiple_of(pair * LANES, LANES), LANES), :] = jnp.transpose(leaving)
+                s_buf[pl.ds(pl.multiple_of(pair * LANES, LANES), LANES), :] = jnp.transpose(
+                    z_out[pair]
+                )
 
     def finish(group):
         ones2 = head_ones()
@@ -275,8 +279,6 @@
         @pl.when(s == 0)
         def _():
             pl.semaphore_wait(barrier, members - 1)
-            for copy in gain_copies:
-                copy.wait()
 
         done = s - finish_from
 
@@ -334,10 +336,10 @@
             jax.ShapeDtypeStruct((T, channels), BF16),
             jax.ShapeDtypeStruct((share, C), F32),
         ),
-        in_specs=[pl.BlockSpec(memory_space=pl.ANY)] * 8,
+        in_specs=[pl.BlockSpec(memory_space=pltpu.HBM)] * 6
+        + [pl.BlockSpec(memory_space=pltpu.VMEM)] * 2,
         out_specs=[pl.BlockSpec(memory_space=pltpu.VMEM)] * 2,
         scratch_shapes=[pltpu.VMEM((T, channels), BF16)] * 6
-        + [pltpu.VMEM((1, channels), F32)] * 2
         + [
             pltpu.VMEM((pairs, T + C, LANES), F32),
             pltpu.VMEM((pairs, T + C, LANES), F32),
@@ -350,10 +352,9 @@
             pltpu.SemaphoreType.DMA,
             pltpu.SemaphoreType.DMA,
             pltpu.SemaphoreType.DMA((6, pairs // GROUP)),
-            pltpu.SemaphoreType.DMA((2,)),
         ],
         compiler_params=pltpu.CompilerParams(
-            collective_id=0, has_side_effects=True, vmem_limit_bytes=60 * 1024 * 1024
+            collective_id=0, has_side_effects=True, vmem_limit_bytes=40 * 1024 * 1024
         ),
     )
     out, final = call(

time: 39 us -> 41.3 us (1.059)
  local copies, waits for them, and re-layouts: 5.27 us -> 8.01 us
  Pallas kernels: 32.8 us -> 32.2 us
    unnamed x6 -> x18, local copies, waits for them, and re-layouts: 4.07 us -> 8 us
    pallas_call x1, Pallas kernels: 32.8 us -> 32.2 us  [on_device(): call(*(x.reshape(T, channels) for x in (r, lf, k, v, e, a)), u.reshape(1,...]
    reshape x1, local copies, waits for them, and re-layouts: 0.6 us -> 0.01 us  [on_device(): g.reshape(1, channels)]
    reshape x1, local copies, waits for them, and re-layouts: 0.6 us -> 0.01 us  [on_device(): u.reshape(1, channels)]
where the time goes in v3:
time: 41.3 us; the launch traced here: 40.9 us
  Pallas kernels  32.2 us (78%)
  local copies, waits for them, and re-layouts  8.01 us (19%)
  between operations  0.67 us (2%)
    pallas_call x1, Pallas kernels, on_device(): call(*(x.reshape(T, channels) for x in (r, lf, k, v, e, a)), u.reshape(1,...  32.2 us
    unnamed x18, local copies, waits for them, and re-layouts  8 us

profile of v3, /device:TPU:18, one launch (start us, length us, event | category | flops | bytes accessed | tf_op | source)
XLA Modules:
  0.0 40.9 jit_solution(9861913413528313418)
XLA Ops:
  0.6 0.0 copy-start.6
  0.6 0.0 copy-start.7
  0.6 0.7 %copy-done.6 = f32[1280]{0:T(1024)S(1)} copy-done((f32[1280]{0:T(1024)S(1)}, f32[1280]{0:T(1024)}, u32[]{:S(2)}) %copy-start.6) | copy-done | bytes 5144
  1.3 0.0 copy-done.7
  1.3 0.0 copy-start
  1.4 1.0 %copy-done = bf16[1,128,1280]{2,1,0:T(8,128)(2,1)S(1)} copy-done((bf16[1,128,1280]{2,1,0:T(8,128)(2,1)S(1)}, bf16[1,128,1280]{2,1,0:T(8,128)(2,1)}, u32[]{:S(2)}) %copy-start) | copy-done | bytes 327704
  2.3 0.0 copy-start.1
  2.3 1.0 %copy-done.1 = bf16[1,128,1280]{2,1,0:T(8,128)(2,1)S(1)} copy-done((bf16[1,128,1280]{2,1,0:T(8,128)(2,1)S(1)}, bf16[1,128,1280]{2,1,0:T(8,128)(2,1)}, u32[]{:S(2)}) %copy-start.1) | copy-done | bytes 327704
  3.3 0.0 copy-start.2
  3.3 1.0 %copy-done.2 = bf16[1,128,1280]{2,1,0:T(8,128)(2,1)S(1)} copy-done((bf16[1,128,1280]{2,1,0:T(8,128)(2,1)S(1)}, bf16[1,128,1280]{2,1,0:T(8,128)(2,1)}, u32[]{:S(2)}) %copy-start.2) | copy-done | bytes 327704
  4.3 0.0 copy-start.3
  4.3 1.0 %copy-done.3 = bf16[1,128,1280]{2,1,0:T(8,128)(2,1)S(1)} copy-done((bf16[1,128,1280]{2,1,0:T(8,128)(2,1)S(1)}, bf16[1,128,1280]{2,1,0:T(8,128)(2,1)}, u32[]{:S(2)}) %copy-start.3) | copy-done | bytes 327704
  5.2 0.0 copy-start.4
  5.2 1.0 %copy-done.4 = bf16[1,128,1280]{2,1,0:T(8,128)(2,1)S(1)} copy-done((bf16[1,128,1280]{2,1,0:T(8,128)(2,1)S(1)}, bf16[1,128,1280]{2,1,0:T(8,128)(2,1)}, u32[]{:S(2)}) %copy-start.4) | copy-done | bytes 327704
  6.2 0.0 copy-start.5
  6.2 1.0 %copy-done.5 = bf16[1,128,1280]{2,1,0:T(8,128)(2,1)S(1)} copy-done((bf16[1,128,1280]{2,1,0:T(8,128)(2,1)S(1)}, bf16[1,128,1280]{2,1,0:T(8,128)(2,1)}, u32[]{:S(2)}) %copy-start.5) | copy-done | bytes 327704
  7.2 32.2 %shard_map.95 = (bf16[128,1280]{1,0:T(8,128)(2,1)S(1)}, f32[320,64]{1,0:T(8,128)S(1)}) custom-call(bf16[128,1280]{1,0:T(8,128)(2,1)S(1)} %bitcast.9, bf16[128,1280]{1,0:T(8,128)(2,1)S(1)} %bitcast.10, bf16[128,1280]{1,0:T(8,128)(2,1)S(1)} %bitcast.11, bf16[128,1280]{1,0:T(8,128)(2,1)S(1)} %bitcast.12, bf16[128,1280]{1,0:T(8,128)(2,1)S(1)} %bitcast.13, ...), custom_call_target="tpu_custom_call" | custom-call | tf_op jit(solution)/shard_map/pallas_call | solution.py:360
  39.4 0.8 %copy.10 = f32[1,320,64]{1,2,0:T(8,128)} copy(f32[1,320,64]{2,1,0:T(8,128)S(1)} %bitcast.15) | data formatting | bytes 163840
  40.2 0.7 %copy.12 = bf16[1,128,1280]{2,1,0:T(8,128)(2,1)} copy(bf16[1,128,1280]{2,1,0:T(8,128)(2,1)S(1)} %bitcast.8) | data formatting | bytes 655360
  (2 shorter events, 0.0 us)
Async XLA Ops:
  0.6 0.7 %copy-start.6 = (f32[1280]{0:T(1024)S(1)}, f32[1280]{0:T(1024)}, u32[]{:S(2)}) copy-start(f32[1280]{0:T(1024)} %param.14) | copy-start | bytes 15364
  0.6 0.7 %copy-start.7 = (f32[1280]{0:T(1024)S(1)}, f32[1280]{0:T(1024)}, u32[]{:S(2)}) copy-start(f32[1280]{0:T(1024)} %param.15) | copy-start | bytes 15364
  1.3 1.0 %copy-start = (bf16[1,128,1280]{2,1,0:T(8,128)(2,1)S(1)}, bf16[1,128,1280]{2,1,0:T(8,128)(2,1)}, u32[]{:S(2)}) copy-start(bf16[1,128,1280]{2,1,0:T(8,128)(2,1)} %param.8) | copy-start | bytes 983044
  2.3 1.0 %copy-start.1 = (bf16[1,128,1280]{2,1,0:T(8,128)(2,1)S(1)}, bf16[1,128,1280]{2,1,0:T(8,128)(2,1)}, u32[]{:S(2)}) copy-start(bf16[1,128,1280]{2,1,0:T(8,128)(2,1)} %param.9) | copy-start | bytes 983044
  3.3 1.0 %copy-start.2 = (bf16[1,128,1280]{2,1,0:T(8,128)(2,1)S(1)}, bf16[1,128,1280]{2,1,0:T(8,128)(2,1)}, u32[]{:S(2)}) copy-start(bf16[1,128,1280]{2,1,0:T(8,128)(2,1)} %param.10) | copy-start | bytes 983044
  4.3 1.0 %copy-start.3 = (bf16[1,128,1280]{2,1,0:T(8,128)(2,1)S(1)}, bf16[1,128,1280]{2,1,0:T(8,128)(2,1)}, u32[]{:S(2)}) copy-start(bf16[1,128,1280]{2,1,0:T(8,128)(2,1)} %param.11) | copy-start | bytes 983044
  5.2 1.0 %copy-start.4 = (bf16[1,128,1280]{2,1,0:T(8,128)(2,1)S(1)}, bf16[1,128,1280]{2,1,0:T(8,128)(2,1)}, u32[]{:S(2)}) copy-start(bf16[1,128,1280]{2,1,0:T(8,128)(2,1)} %param.12) | copy-start | bytes 983044
  6.2 1.0 %copy-start.5 = (bf16[1,128,1280]{2,1,0:T(8,128)(2,1)S(1)}, bf16[1,128,1280]{2,1,0:T(8,128)(2,1)}, u32[]{:S(2)}) copy-start(bf16[1,128,1280]{2,1,0:T(8,128)(2,1)} %param.13) | copy-start | bytes 983044

commit v4 on v3

--- a/solution.py
+++ b/solution.py
@@ -12,7 +12,9 @@
 KEY_EPS = 1e-05
 NORM_EPS = 0.00064
 FINE_LEVELS = 3
-GROUP = 5
+GROUP = 2
+PIECES = 4
+VMEM_GRANT = 60 * 1024 * 1024
 F32 = jnp.float32
 BF16 = jnp.bfloat16
 MESH = pl.DeviceIdType.MESH
@@ -64,11 +66,11 @@
 
 def kernel(
     members,
-    r_in, lf_in, k_in, v_in, e_in, a_in, u_ref, g_ref,
-    out_ref, final_ref,
-    r_ref, lf_ref, k_ref, v_ref, e_ref, a_ref,
+    r_in, lf_in, k_in, v_in, e_in, a_in, u_in, g_in,
+    out_hbm, final_ref,
+    r_ref, lf_ref, k_ref, v_ref, e_ref, a_ref, u_ref, g_ref, out_ref,
     w_buf, add_buf, z_in, z_out, s_buf,
-    send_sem, recv_sem, fsend_sem, frecv_sem, local_sem, in_sem,
+    send_sem, recv_sem, fsend_sem, frecv_sem, local_sem, in_sem, gain_sem, out_sem,
 ):
     T, channels = r_ref.shape
     pairs = channels // LANES
@@ -96,6 +98,12 @@
     for group in range(groups):
         for copy in input_copies(group):
             copy.start()
+    gain_copies = [
+        pltpu.make_async_copy(source, target, gain_sem.at[i])
+        for i, (source, target) in enumerate(((u_in, u_ref), (g_in, g_ref)))
+    ]
+    for copy in gain_copies:
+        copy.start()
 
     @pl.when(me == 0)
     def _():
@@ -146,14 +154,22 @@
             vroll = pltpu.roll(v_ref[:, at].astype(F32), C, 1)
             vroll_b = vroll.astype(BF16)
             vroll2 = cat([vroll_b, vroll_b], 0)
-            qhi, qlo = split(cat([toward, reader], 0))
-            q3 = cat([qhi, qlo, qhi], 1)
+            first2 = lane_ids(2 * T) < C
+            query = cat([toward, reader], 0)
+            qhi = query.astype(BF16)
+            qlo_r = pltpu.roll(query - qhi.astype(F32), C, 1).astype(BF16)
+            sides = cat([away, keys], 0)
+            khi = sides.astype(BF16)
+            klo = (sides - khi.astype(F32)).astype(BF16)
+            khi_r = pltpu.roll(khi.astype(F32), C, 1).astype(BF16)
             ends.append((reader_true, jnp.where(diag, gamma, 0.0)))
             for h in range(2):
                 own = first if h == 0 else jnp.logical_not(first)
-                sides = cat([jnp.where(own, away, 0.0), jnp.where(own, keys, 0.0)], 0)
-                khi, klo = split(sides)
-                scores = dot_t(q3, cat([khi, khi, klo], 1))
+                own2 = first2 if h == 0 else jnp.logical_not(first2)
+                scores = dot_t(
+                    cat([jnp.where(own2, qhi, qlo_r), qhi], 1),
+                    cat([jnp.where(own2, khi, khi_r), jnp.where(own2, klo, jnp.zeros_like(klo))], 1),
+                )
                 mix_away = jnp.where(strict, scores[:T, :T], 0.0)
                 mix_keys = jnp.where(strict, scores[:T, T:], 0.0)
                 read = cat(
@@ -240,6 +256,10 @@
                     z_out[pair]
                 )
 
+    def out_copy(group):
+        at = pl.ds(pl.multiple_of(group * (GROUP * LANES), LANES), GROUP * LANES)
+        return pltpu.make_async_copy(out_ref.at[:, at], out_hbm.at[:, at], out_sem.at[group])
+
     def finish(group):
         ones2 = head_ones()
         for j in range(GROUP):
@@ -250,10 +270,11 @@
             average = head_sum(result, ones2) * (1.0 / C)
             centered = result - average
             spread = head_sum(centered * centered, ones2) * (1.0 / C)
-            normed = centered * lax.rsqrt(spread + NORM_EPS) * g_ref[:, at]
-            bonus = r_ref[:, at].astype(F32) * k_ref[:, at].astype(F32) * u_ref[:, at]
+            normed = centered * lax.rsqrt(spread + NORM_EPS) * g_ref[at][None, :]
+            bonus = r_ref[:, at].astype(F32) * k_ref[:, at].astype(F32) * u_ref[at][None, :]
             extra = head_sum(bonus, ones2) * v_ref[:, at].astype(F32)
             out_ref[:, at] = (normed + extra).astype(out_ref.dtype)
+        out_copy(group).start()
 
     def final_copy(target):
         return pltpu.make_async_remote_copy(
@@ -279,6 +300,8 @@
         @pl.when(s == 0)
         def _():
             pl.semaphore_wait(barrier, members - 1)
+            for copy in gain_copies:
+                copy.wait()
 
         done = s - finish_from
 
@@ -308,6 +331,9 @@
         return 0
 
     lax.fori_loop(0, groups + max(groups, members), step, 0)
+
+    for group in range(groups):
+        out_copy(group).wait()
 
     @pl.when(me == last)
     def _():
@@ -324,6 +350,28 @@
             return 0
 
         lax.fori_loop(0, pairs, sent, 0)
+
+
+def hand_on(out_in, final_in, out, final, rows, turned, out_sem, final_sem):
+    T = out.shape[0]
+    size = T // PIECES
+    arriving = pltpu.make_async_copy(final_in, rows, final_sem.at[0])
+    arriving.start()
+    pieces = [
+        pltpu.make_async_copy(
+            out_in.at[pl.ds(i * size, size), :], out.at[pl.ds(i * size, size), :], out_sem.at[i]
+        )
+        for i in range(PIECES)
+    ]
+    for piece in pieces:
+        piece.start()
+    arriving.wait()
+    turned[...] = jnp.transpose(rows[...])
+    leaving = pltpu.make_async_copy(turned, final, final_sem.at[1])
+    leaving.start()
+    for piece in pieces:
+        piece.wait()
+    leaving.wait()
 
 
 def on_device(r, lf, k, v, e, a, u, g, *, members):
@@ -336,10 +384,11 @@
             jax.ShapeDtypeStruct((T, channels), BF16),
             jax.ShapeDtypeStruct((share, C), F32),
         ),
-        in_specs=[pl.BlockSpec(memory_space=pltpu.HBM)] * 6
-        + [pl.BlockSpec(memory_space=pltpu.VMEM)] * 2,
-        out_specs=[pl.BlockSpec(memory_space=pltpu.VMEM)] * 2,
+        in_specs=[pl.BlockSpec(memory_space=pl.ANY)] * 8,
+        out_specs=[pl.BlockSpec(memory_space=pl.ANY), pl.BlockSpec(memory_space=pltpu.VMEM)],
         scratch_shapes=[pltpu.VMEM((T, channels), BF16)] * 6
+        + [pltpu.VMEM((channels,), F32)] * 2
+        + [pltpu.VMEM((T, channels), BF16)]
         + [
             pltpu.VMEM((pairs, T + C, LANES), F32),
             pltpu.VMEM((pairs, T + C, LANES), F32),
@@ -352,17 +401,35 @@
             pltpu.SemaphoreType.DMA,
             pltpu.SemaphoreType.DMA,
             pltpu.SemaphoreType.DMA((6, pairs // GROUP)),
+            pltpu.SemaphoreType.DMA((2,)),
+            pltpu.SemaphoreType.DMA((pairs // GROUP,)),
         ],
         compiler_params=pltpu.CompilerParams(
-            collective_id=0, has_side_effects=True, vmem_limit_bytes=40 * 1024 * 1024
+            collective_id=0, has_side_effects=True, vmem_limit_bytes=VMEM_GRANT
         ),
     )
     out, final = call(
         *(x.reshape(T, channels) for x in (r, lf, k, v, e, a)),
-        u.reshape(1, channels),
-        g.reshape(1, channels),
+        u,
+        g,
     )
-    return out.reshape(sequences, T, channels), final.reshape(sequences, share, C)
+    out, final = pl.pallas_call(
+        hand_on,
+        out_shape=(
+            jax.ShapeDtypeStruct((T, channels), BF16),
+            jax.ShapeDtypeStruct((C, share), F32),
+        ),
+        in_specs=[pl.BlockSpec(memory_space=pl.ANY)] * 2,
+        out_specs=[pl.BlockSpec(memory_space=pl.ANY)] * 2,
+        scratch_shapes=[
+            pltpu.VMEM((share, C), F32),
+            pltpu.VMEM((C, share), F32),
+            pltpu.SemaphoreType.DMA((PIECES,)),
+            pltpu.SemaphoreType.DMA((2,)),
+        ],
+        compiler_params=pltpu.CompilerParams(vmem_limit_bytes=VMEM_GRANT),
+    )(out, final)
+    return out.reshape(sequences, T, channels), jnp.transpose(final).reshape(sequences, share, C)
 
 
 def solution(mesh):

time: 41.3 us -> 44.1 us (1.068)
  Pallas kernels: 32.2 us -> 43.3 us
  local copies, waits for them, and re-layouts: 8.01 us -> 0 us
    pallas_call x1 -> x2, Pallas kernels: 32.2 us -> 43.3 us  [the longest x1 32.2 us: on_device(): call(*(x.reshape(T, channels) for x in (r, lf, k, v, e, a)), u, g)]
    unnamed x18 -> x0, local copies, waits for them, and re-layouts: 8 us -> none
where the time goes in v4:
time: 44.1 us; the launch traced here: 43.9 us
  Pallas kernels  43.3 us (98%)
  between operations  0.64 us (1%)
    pallas_call x1, Pallas kernels, on_device(): call(*(x.reshape(T, channels) for x in (r, lf, k, v, e, a)), u, g)  32.2 us
    pallas_call x1, Pallas kernels, on_device(): pl.pallas_call(hand_on, out_shape=(jax.ShapeDtypeStruct((T, channels), BF...  11.1 us

profile of v4, /device:TPU:18, one launch (start us, length us, event | category | flops | bytes accessed | tf_op | source)
XLA Modules:
  0.0 43.9 jit_solution(10322126102800044049)
XLA Ops:
  0.6 32.2 %shard_map.95 = (bf16[128,1280]{1,0:T(8,128)(2,1)}, f32[320,64]{1,0:T(8,128)}) custom-call(bf16[128,1280]{1,0:T(8,128)(2,1)} %bitcast.10, bf16[128,1280]{1,0:T(8,128)(2,1)} %bitcast.11, bf16[128,1280]{1,0:T(8,128)(2,1)} %bitcast.12, bf16[128,1280]{1,0:T(8,128)(2,1)} %bitcast.13, bf16[128,1280]{1,0:T(8,128)(2,1)} %bitcast.14, bf16[128,1280]{1,0:T(8,128)(2,1)} %bitcast.15, ...), custom_call_target="tpu_custom_call" | custom-call | tf_op jit(solution)/shard_map/pallas_call | solution.py:411
  32.8 11.1 %shard_map.96 = (bf16[128,1280]{1,0:T(8,128)(2,1)}, f32[64,320]{1,0:T(8,128)}) custom-call(bf16[128,1280]{1,0:T(8,128)(2,1)} %get-tuple-element.6.out_in, f32[320,64]{1,0:T(8,128)} %get-tuple-element.7.final_in), custom_call_target="tpu_custom_call" | custom-call | tf_op jit(solution)/shard_map/pallas_call | solution.py:416

commit v5 on v4

--- a/solution.py
+++ b/solution.py
@@ -46,6 +46,29 @@
     return dot(cat([hi, lo], 1), ones2)
 
 
+def split_rolled(x):
+    hi = x.astype(BF16)
+    return hi, pltpu.roll(x - hi.astype(F32), C, 1).astype(BF16)
+
+
+def head_scores(h, qhi, qlo_r, khi, khi_r, klo):
+    q_first = lane_ids(qhi.shape[0]) < C
+    k_first = lane_ids(khi.shape[0]) < C
+    if h == 1:
+        q_first, k_first = jnp.logical_not(q_first), jnp.logical_not(k_first)
+    return dot_t(
+        cat([jnp.where(q_first, qhi, qlo_r), qhi], 1),
+        cat([jnp.where(k_first, khi, khi_r), jnp.where(k_first, klo, jnp.zeros_like(klo))], 1),
+    )
+
+
+def through_solve(left, x, v):
+    lhi, llo = split(left)
+    xhi, xlo = split(x)
+    rhi = cat([xhi, v], 0)
+    return dot(cat([lhi, llo, lhi[:, : x.shape[0]]], 1), cat([rhi, rhi, xlo], 0))
+
+
 def head_ones():
     rows = lax.broadcasted_iota(jnp.int32, (2 * LANES, LANES), 0)
     cols = lax.broadcasted_iota(jnp.int32, (2 * LANES, LANES), 1)
@@ -69,7 +92,7 @@
     r_in, lf_in, k_in, v_in, e_in, a_in, u_in, g_in,
     out_hbm, final_ref,
     r_ref, lf_ref, k_ref, v_ref, e_ref, a_ref, u_ref, g_ref, out_ref,
-    w_buf, add_buf, z_in, z_out, s_buf,
+    reader_buf, sides_buf, x_buf, w_buf, add_buf, z_in, z_out, s_buf,
     send_sem, recv_sem, fsend_sem, frecv_sem, local_sem, in_sem, gain_sem, out_sem,
 ):
     T, channels = r_ref.shape
@@ -117,12 +140,11 @@
             copy.wait()
         rows = lax.broadcasted_iota(jnp.int32, (T, T), 0)
         cols = lax.broadcasted_iota(jnp.int32, (T, T), 1)
-        inclusive = rows >= cols
         strict = rows > cols
-        lower = jnp.where(inclusive, 1.0, 0.0).astype(BF16)
+        lower = jnp.where(rows >= cols, 1.0, 0.0).astype(BF16)
         first = lane_ids(T) < C
         ones2 = head_ones()
-        state_lanes = lane_ids(T + C) < C
+        state_lanes = lane_ids(C) < C
         diag = lax.rem(lane_ids(C), C) == lax.broadcasted_iota(jnp.int32, (C, LANES), 0)
         heads = []
         ends = []
@@ -154,39 +176,32 @@
             vroll = pltpu.roll(v_ref[:, at].astype(F32), C, 1)
             vroll_b = vroll.astype(BF16)
             vroll2 = cat([vroll_b, vroll_b], 0)
-            first2 = lane_ids(2 * T) < C
-            query = cat([toward, reader], 0)
-            qhi = query.astype(BF16)
-            qlo_r = pltpu.roll(query - qhi.astype(F32), C, 1).astype(BF16)
+            thi, tlo = split_rolled(toward)
+            rhi, rlo = split_rolled(reader)
             sides = cat([away, keys], 0)
             khi = sides.astype(BF16)
             klo = (sides - khi.astype(F32)).astype(BF16)
             khi_r = pltpu.roll(khi.astype(F32), C, 1).astype(BF16)
-            ends.append((reader_true, jnp.where(diag, gamma, 0.0)))
+            pair = group * GROUP + j
+            reader_buf[pair, 0] = rhi
+            reader_buf[pair, 1] = rlo
+            sides_buf[pair, 0] = khi
+            sides_buf[pair, 1] = khi_r
+            sides_buf[pair, 2] = klo
+            w_buf[pair, :T, :] = reader_true
+            ends.append(jnp.where(diag, gamma, 0.0))
             for h in range(2):
                 own = first if h == 0 else jnp.logical_not(first)
-                own2 = first2 if h == 0 else jnp.logical_not(first2)
-                scores = dot_t(
-                    cat([jnp.where(own2, qhi, qlo_r), qhi], 1),
-                    cat([jnp.where(own2, khi, khi_r), jnp.where(own2, klo, jnp.zeros_like(klo))], 1),
-                )
-                mix_away = jnp.where(strict, scores[:T, :T], 0.0)
-                mix_keys = jnp.where(strict, scores[:T, T:], 0.0)
-                read = cat(
-                    [
-                        jnp.where(inclusive, scores[T:, :T], 0.0),
-                        jnp.where(inclusive, scores[T:, T:], 0.0),
-                    ],
-                    1,
-                )
-                closing = cat([away_t[h * C : h * C + C], keys_t[h * C : h * C + C]], 1)
+                scores = head_scores(h, thi, tlo, khi, khi_r, klo)
+                mix_away = jnp.where(strict, scores[:, :T], 0.0)
+                mix_keys = jnp.where(strict, scores[:, T:], 0.0)
                 mhi, mlo = split(mix_keys)
                 mixed = dot(cat([mhi, mlo], 1), vroll2)
                 heads.append(
                     dict(
                         y=mix_away,
                         x=jnp.where(own, toward_true, mixed),
-                        left=cat([read, closing], 0),
+                        left=cat([away_t[h * C : h * C + C], keys_t[h * C : h * C + C]], 1),
                         v=jnp.where(own, 0.0, vroll).astype(BF16),
                     )
                 )
@@ -212,15 +227,36 @@
                 gained = prod[:, -LANES:]
                 head["x"] = cat([x[:skip], x[skip:] + gained], 0) if skip else x + gained
         for j in range(GROUP):
+            pair = group * GROUP + j
             results = []
-            for head in heads[2 * j : 2 * j + 2]:
-                lhi, llo = split(head["left"])
-                xhi, xlo = split(head["x"])
-                rhi = cat([xhi, head["v"]], 0)
-                results.append(dot(cat([lhi, llo, lhi[:, :T]], 1), cat([rhi, rhi, xlo], 0)))
+            for h, head in enumerate(heads[2 * j : 2 * j + 2]):
+                x_buf[pair, h] = head["x"]
+                results.append(through_solve(head["left"], head["x"], head["v"]))
+            w_buf[pair, T:, :] = jnp.where(state_lanes, results[0], results[1]) + ends[j]
+            add_buf[pair, T:, :] = pltpu.roll(
+                jnp.where(state_lanes, results[1], results[0]), C, 1
+            )
+
+    def read(group):
+        rows = lax.broadcasted_iota(jnp.int32, (T, 2 * T), 0)
+        cols = lax.rem(lax.broadcasted_iota(jnp.int32, (T, 2 * T), 1), T)
+        inclusive = rows >= cols
+        first = lane_ids(T) < C
+        for j in range(GROUP):
             pair = group * GROUP + j
-            w_buf[pair] = jnp.where(state_lanes, results[0], results[1]) + cat(list(ends[j]), 0)
-            add_buf[pair] = pltpu.roll(jnp.where(state_lanes, results[1], results[0]), C, 1)
+            vroll = pltpu.roll(v_ref[:, lanes_of(pair)].astype(F32), C, 1)
+            results = []
+            for h in range(2):
+                own = first if h == 0 else jnp.logical_not(first)
+                scores = head_scores(
+                    h, reader_buf[pair, 0], reader_buf[pair, 1],
+                    sides_buf[pair, 0], sides_buf[pair, 1], sides_buf[pair, 2],
+                )
+                own_v = jnp.where(own, 0.0, vroll).astype(BF16)
+                left = jnp.where(inclusive, scores, 0.0)
+                results.append(through_solve(left, x_buf[pair, h], own_v))
+            w_buf[pair, :T, :] += jnp.where(first, results[0], results[1])
+            add_buf[pair, :T, :] = pltpu.roll(jnp.where(first, results[1], results[0]), C, 1)
 
     def state_copy(pair):
         return pltpu.make_async_remote_copy(
@@ -290,7 +326,8 @@
         return pltpu.make_async_copy(s_buf.at[pl.ds(last * share, share), :], final_ref, local_sem)
 
     group_rows = GROUP * LANES
-    finish_from = jnp.maximum(me + 1, groups - (me // last) * groups)
+    read_from = groups - (me // last) * (groups - 1)
+    finish_from = jnp.maximum(me, read_from)
 
     def step(s, _):
         @pl.when(s < groups)
@@ -303,12 +340,6 @@
             for copy in gain_copies:
                 copy.wait()
 
-        done = s - finish_from
-
-        @pl.when(jnp.logical_and(done >= 0, done < groups))
-        def _():
-            finish(done)
-
         turn = s - me
 
         @pl.when(jnp.logical_and(turn >= 0, turn < groups))
@@ -327,6 +358,18 @@
                 @pl.when(turn == groups - 1)
                 def _():
                     own_copy().start()
+
+        ahead = s - read_from
+
+        @pl.when(jnp.logical_and(ahead >= 0, ahead < groups))
+        def _():
+            read(ahead)
+
+        done = s - finish_from
+
+        @pl.when(jnp.logical_and(done >= 0, done < groups))
+        def _():
+            finish(done)
 
         return 0
 
@@ -352,25 +395,31 @@
         lax.fori_loop(0, pairs, sent, 0)
 
 
-def hand_on(out_in, final_in, out, final, rows, turned, out_sem, final_sem):
+def hand_on(out_in, final_in, out, final, rows, turned, held, in_sem, out_sem, final_sem):
     T = out.shape[0]
     size = T // PIECES
     arriving = pltpu.make_async_copy(final_in, rows, final_sem.at[0])
     arriving.start()
-    pieces = [
-        pltpu.make_async_copy(
-            out_in.at[pl.ds(i * size, size), :], out.at[pl.ds(i * size, size), :], out_sem.at[i]
-        )
-        for i in range(PIECES)
+    parts = [pl.ds(i * size, size) for i in range(PIECES)]
+    loads = [
+        pltpu.make_async_copy(out_in.at[at, :], held.at[at, :], in_sem.at[i])
+        for i, at in enumerate(parts)
     ]
-    for piece in pieces:
-        piece.start()
+    stores = [
+        pltpu.make_async_copy(held.at[at, :], out.at[at, :], out_sem.at[i])
+        for i, at in enumerate(parts)
+    ]
+    for load in loads:
+        load.start()
     arriving.wait()
     turned[...] = jnp.transpose(rows[...])
     leaving = pltpu.make_async_copy(turned, final, final_sem.at[1])
     leaving.start()
-    for piece in pieces:
-        piece.wait()
+    for load, store in zip(loads, stores):
+        load.wait()
+        store.start()
+    for store in stores:
+        store.wait()
     leaving.wait()
 
 
@@ -390,6 +439,9 @@
         + [pltpu.VMEM((channels,), F32)] * 2
         + [pltpu.VMEM((T, channels), BF16)]
         + [
+            pltpu.VMEM((pairs, 2, T, LANES), BF16),
+            pltpu.VMEM((pairs, 3, 2 * T, LANES), BF16),
+            pltpu.VMEM((pairs, 2, T, LANES), F32),
             pltpu.VMEM((pairs, T + C, LANES), F32),
             pltpu.VMEM((pairs, T + C, LANES), F32),
             pltpu.VMEM((pairs, C, LANES), F32),
@@ -424,6 +476,8 @@
         scratch_shapes=[
             pltpu.VMEM((share, C), F32),
             pltpu.VMEM((C, share), F32),
+            pltpu.VMEM((T, channels), BF16),
+            pltpu.SemaphoreType.DMA((PIECES,)),
             pltpu.SemaphoreType.DMA((PIECES,)),
             pltpu.SemaphoreType.DMA((2,)),
         ],

time: 44.1 us -> 37.4 us (0.85)
  Pallas kernels: 43.3 us -> 36.5 us
    pallas_call x1, Pallas kernels: 11.1 us -> 1.99 us  [on_device(): pl.pallas_call(hand_on, out_shape=(jax.ShapeDtypeStruct((T, channels), BF...]
    pallas_call x1, Pallas kernels: 32.2 us -> 34.5 us  [on_device(): call(*(x.reshape(T, channels) for x in (r, lf, k, v, e, a)), u, g)]
where the time goes in v5:
time: 37.4 us; the launch traced here: 37.2 us
  Pallas kernels  36.5 us (98%)
  between operations  0.64 us (2%)
    pallas_call x1, Pallas kernels, on_device(): call(*(x.reshape(T, channels) for x in (r, lf, k, v, e, a)), u, g)  34.5 us
    pallas_call x1, Pallas kernels, on_device(): pl.pallas_call(hand_on, out_shape=(jax.ShapeDtypeStruct((T, channels), BF...  1.99 us

profile of v5, /device:TPU:18, one launch (start us, length us, event | category | flops | bytes accessed | tf_op | source)
XLA Modules:
  0.0 37.2 jit_solution(748613322472735801)
XLA Ops:
  0.6 34.5 %shard_map.95 = (bf16[128,1280]{1,0:T(8,128)(2,1)}, f32[320,64]{1,0:T(8,128)}) custom-call(bf16[128,1280]{1,0:T(8,128)(2,1)} %bitcast.10, bf16[128,1280]{1,0:T(8,128)(2,1)} %bitcast.11, bf16[128,1280]{1,0:T(8,128)(2,1)} %bitcast.12, bf16[128,1280]{1,0:T(8,128)(2,1)} %bitcast.13, bf16[128,1280]{1,0:T(8,128)(2,1)} %bitcast.14, bf16[128,1280]{1,0:T(8,128)(2,1)} %bitcast.15, ...), custom_call_target="tpu_custom_call" | custom-call | tf_op jit(solution)/shard_map/pallas_call | solution.py:463
  35.2 2.0 %shard_map.96 = (bf16[128,1280]{1,0:T(8,128)(2,1)}, f32[64,320]{1,0:T(8,128)}) custom-call(bf16[128,1280]{1,0:T(8,128)(2,1)} %get-tuple-element.6.out_in, f32[320,64]{1,0:T(8,128)} %get-tuple-element.7.final_in), custom_call_target="tpu_custom_call" | custom-call | tf_op jit(solution)/shard_map/pallas_call | solution.py:468

commit v6 on v4

--- a/solution.py
+++ b/solution.py
@@ -352,25 +352,31 @@
         lax.fori_loop(0, pairs, sent, 0)
 
 
-def hand_on(out_in, final_in, out, final, rows, turned, out_sem, final_sem):
+def hand_on(out_in, final_in, out, final, rows, turned, held, in_sem, out_sem, final_sem):
     T = out.shape[0]
     size = T // PIECES
     arriving = pltpu.make_async_copy(final_in, rows, final_sem.at[0])
     arriving.start()
-    pieces = [
-        pltpu.make_async_copy(
-            out_in.at[pl.ds(i * size, size), :], out.at[pl.ds(i * size, size), :], out_sem.at[i]
-        )
-        for i in range(PIECES)
+    parts = [pl.ds(i * size, size) for i in range(PIECES)]
+    loads = [
+        pltpu.make_async_copy(out_in.at[at, :], held.at[at, :], in_sem.at[i])
+        for i, at in enumerate(parts)
     ]
-    for piece in pieces:
-        piece.start()
+    stores = [
+        pltpu.make_async_copy(held.at[at, :], out.at[at, :], out_sem.at[i])
+        for i, at in enumerate(parts)
+    ]
+    for load in loads:
+        load.start()
     arriving.wait()
     turned[...] = jnp.transpose(rows[...])
     leaving = pltpu.make_async_copy(turned, final, final_sem.at[1])
     leaving.start()
-    for piece in pieces:
-        piece.wait()
+    for load, store in zip(loads, stores):
+        load.wait()
+        store.start()
+    for store in stores:
+        store.wait()
     leaving.wait()
 
 
@@ -424,6 +430,8 @@
         scratch_shapes=[
             pltpu.VMEM((share, C), F32),
             pltpu.VMEM((C, share), F32),
+            pltpu.VMEM((T, channels), BF16),
+            pltpu.SemaphoreType.DMA((PIECES,)),
             pltpu.SemaphoreType.DMA((PIECES,)),
             pltpu.SemaphoreType.DMA((2,)),
         ],

time: 44.1 us -> 35 us (0.79)
  Pallas kernels: 43.3 us -> 34.2 us
    pallas_call x1, Pallas kernels: 11.1 us -> 1.99 us  [on_device(): pl.pallas_call(hand_on, out_shape=(jax.ShapeDtypeStruct((T, channels), BF...]
where the time goes in v6:
time: 35 us; the launch traced here: 34.8 us
  Pallas kernels  34.2 us (98%)
  between operations  0.64 us (2%)
    pallas_call x1, Pallas kernels, on_device(): call(*(x.reshape(T, channels) for x in (r, lf, k, v, e, a)), u, g)  32.2 us
    pallas_call x1, Pallas kernels, on_device(): pl.pallas_call(hand_on, out_shape=(jax.ShapeDtypeStruct((T, channels), BF...  1.99 us

profile of v6, /device:TPU:18, one launch (start us, length us, event | category | flops | bytes accessed | tf_op | source)
XLA Modules:
  0.0 34.8 jit_solution(10942341951164313401)
XLA Ops:
  0.6 32.2 %shard_map.95 = (bf16[128,1280]{1,0:T(8,128)(2,1)}, f32[320,64]{1,0:T(8,128)}) custom-call(bf16[128,1280]{1,0:T(8,128)(2,1)} %bitcast.10, bf16[128,1280]{1,0:T(8,128)(2,1)} %bitcast.11, bf16[128,1280]{1,0:T(8,128)(2,1)} %bitcast.12, bf16[128,1280]{1,0:T(8,128)(2,1)} %bitcast.13, bf16[128,1280]{1,0:T(8,128)(2,1)} %bitcast.14, bf16[128,1280]{1,0:T(8,128)(2,1)} %bitcast.15, ...), custom_call_target="tpu_custom_call" | custom-call | tf_op jit(solution)/shard_map/pallas_call | solution.py:417
  32.8 2.0 %shard_map.96 = (bf16[128,1280]{1,0:T(8,128)(2,1)}, f32[64,320]{1,0:T(8,128)}) custom-call(bf16[128,1280]{1,0:T(8,128)(2,1)} %get-tuple-element.6.out_in, f32[320,64]{1,0:T(8,128)} %get-tuple-element.7.final_in), custom_call_target="tpu_custom_call" | custom-call | tf_op jit(solution)/shard_map/pallas_call | solution.py:422

commit v7 on v6

--- a/solution.py
+++ b/solution.py
@@ -233,28 +233,31 @@
         )
 
     def relay(group):
-        for j in range(GROUP):
-            pair = group * GROUP + j
-
-            @pl.when(me == 0)
-            def _():
+        pairs_now = [group * GROUP + j for j in range(GROUP)]
+
+        @pl.when(me == 0)
+        def _():
+            for pair in pairs_now:
                 z_out[pair] = add_buf[pair, T:, :]
 
-            @pl.when(me > 0)
-            def _():
+        @pl.when(me > 0)
+        def _():
+            for pair in pairs_now:
                 state_copy(pair).wait_recv()
-                z = diagonal_state(z_in[pair])
-                z_out[pair] = product3(w_buf[pair, T:, :], z) + add_buf[pair, T:, :]
-
-            @pl.when(me < last)
-            def _():
+            states = [diagonal_state(z_in[pair]) for pair in pairs_now]
+            moved = [product3(w_buf[pair, T:, :], z) for pair, z in zip(pairs_now, states)]
+            for pair, product in zip(pairs_now, moved):
+                z_out[pair] = product + add_buf[pair, T:, :]
+
+        @pl.when(me < last)
+        def _():
+            for pair in pairs_now:
                 state_copy(pair).start()
 
-            @pl.when(me == last)
-            def _():
-                s_buf[pl.ds(pl.multiple_of(pair * LANES, LANES), LANES), :] = jnp.transpose(
-                    z_out[pair]
-                )
+        @pl.when(me == last)
+        def _():
+            for pair in pairs_now:
+                s_buf[lanes_of(pair), :] = jnp.transpose(z_out[pair])
 
     def out_copy(group):
         at = pl.ds(pl.multiple_of(group * (GROUP * LANES), LANES), GROUP * LANES)

time: 35 us -> 34.6 us (0.989)
  Pallas kernels: 34.2 us -> 33.8 us
    pallas_call x1, Pallas kernels: 32.2 us -> 31.8 us  [on_device(): call(*(x.reshape(T, channels) for x in (r, lf, k, v, e, a)), u, g)]
where the time goes in v7:
time: 34.6 us; the launch traced here: 34.4 us
  Pallas kernels  33.8 us (98%)
  between operations  0.64 us (2%)
    pallas_call x1, Pallas kernels, on_device(): call(*(x.reshape(T, channels) for x in (r, lf, k, v, e, a)), u, g)  31.8 us
    pallas_call x1, Pallas kernels, on_device(): pl.pallas_call(hand_on, out_shape=(jax.ShapeDtypeStruct((T, channels), BF...  1.99 us

profile of v7, /device:TPU:18, one launch (start us, length us, event | category | flops | bytes accessed | tf_op | source)
XLA Modules:
  0.0 34.4 jit_solution(15357817602129666509)
XLA Ops:
  0.6 31.8 %shard_map.95 = (bf16[128,1280]{1,0:T(8,128)(2,1)}, f32[320,64]{1,0:T(8,128)}) custom-call(bf16[128,1280]{1,0:T(8,128)(2,1)} %bitcast.10, bf16[128,1280]{1,0:T(8,128)(2,1)} %bitcast.11, bf16[128,1280]{1,0:T(8,128)(2,1)} %bitcast.12, bf16[128,1280]{1,0:T(8,128)(2,1)} %bitcast.13, bf16[128,1280]{1,0:T(8,128)(2,1)} %bitcast.14, bf16[128,1280]{1,0:T(8,128)(2,1)} %bitcast.15, ...), custom_call_target="tpu_custom_call" | custom-call | tf_op jit(solution)/shard_map/pallas_call | solution.py:420
  32.4 2.0 %shard_map.96 = (bf16[128,1280]{1,0:T(8,128)(2,1)}, f32[64,320]{1,0:T(8,128)}) custom-call(bf16[128,1280]{1,0:T(8,128)(2,1)} %get-tuple-element.6.out_in, f32[320,64]{1,0:T(8,128)} %get-tuple-element.7.final_in), custom_call_target="tpu_custom_call" | custom-call | tf_op jit(solution)/shard_map/pallas_call | solution.py:425
